TPU v7x, 32 devices: a whole 2x2x4 slice. The times are simulated.
32 devices in a mesh: tok: 8 (over z, x), head: 4 (over y, core).
Axes of the slice: x: 2, y: 2, z: 4, core: 2. Of those that a mesh axis runs over, the one named last changes fastest.
Arguments:
- queries_first: bfloat16 [2048, 3072], P('tok', 'head'), may hold values from -180 to 180
- queries_second: bfloat16 [2048, 3072], P('tok', 'head'), may hold values from -180 to 180
- grads_first: bfloat16 [2048, 3072], P('tok', 'head'), may hold values from -6 to 6
- grads_second: bfloat16 [2048, 3072], P('tok', 'head'), may hold values from -6 to 6
- key_states: bfloat16 [2048, 1024], P('tok', 'head'), may hold values from -4.5 to 4.5
- value_states: bfloat16 [2048, 1024], P('tok', 'head'), may hold values from -6 to 6
- doc_lengths: int32 [8], replicated, may hold values from 1 to 768, 2048 in all
- hidden_states: bfloat16 [2048, 3072], P('tok', 'head'), may hold values from -6 to 6
Outputs:
- grad_queries_first: bfloat16 [2048, 3072], P('tok', 'head')
- grad_queries_second: bfloat16 [2048, 3072], P('tok', 'head')
- weight_grad: float32 [3072, 2048], P('tok', 'head')
All inputs are finite; a program needn't handle non-finite values.
Results may differ from a plain program's by a relative error of at most 0.0075.
Values may be sent and summed in bfloat16 or wider, within the bound.
No kernel may reach another device: no remote copies, remote signals or barrier semaphores. Data moves between devices by JAX's collectives and lax.ppermute only.
A program may use at most 64 MiB of HBM per device.

v0:
```python
import math

import jax
import jax.numpy as jnp
from jax import lax
from jax.sharding import PartitionSpec as P

HD = 128
REACH = 3


def passed_along(value, axis, steps):
    count = lax.axis_size(axis)
    initial, last = (max(0, -steps), min(count, count - steps))
    return lax.ppermute(value, axis, [(source, source + steps) for source in range(initial, last)])


def document_of(places, doc_ends):
    return jnp.sum((places[:, None] >= doc_ends[None, :]).astype(jnp.int32), axis=1)


def causal_mask(query_places, key_places, doc_ends):
    same_doc = (
        document_of(query_places, doc_ends)[:, None]
        == document_of(jnp.maximum(key_places, 0), doc_ends)[None, :]
    )
    return same_doc & (key_places[None, :] <= query_places[:, None]) & (key_places[None, :] >= 0)


def attend_grads(queries, grad_rows, key_window, value_window, allowed):
    query_rows = queries.shape[0]
    window = key_window.shape[0]
    kv_heads = key_window.shape[1] // HD
    group_size = queries.shape[1] // (kv_heads * HD)
    score_scale = 1.0 / math.sqrt(HD)
    q_four = queries.reshape(query_rows, kv_heads, group_size, HD)
    g_four = grad_rows.reshape(query_rows, kv_heads, group_size, HD)
    k_three = key_window.reshape(window, kv_heads, HD)
    v_three = value_window.reshape(window, kv_heads, HD)
    scores = (
        jnp.einsum("bhgd,whd->hgbw", q_four, k_three, preferred_element_type=jnp.float32)
        * score_scale
    )
    scores = jnp.where(allowed, scores, -1e30)
    row_max = jnp.max(scores, axis=-1, keepdims=True)
    raised = jnp.exp(scores - row_max)
    prob_rows = raised / jnp.sum(raised, axis=-1, keepdims=True)
    prob_half = prob_rows.astype(jnp.bfloat16)
    outputs = jnp.einsum("hgbw,whd->bhgd", prob_half, v_three, preferred_element_type=jnp.float32)
    deltas = jnp.sum(g_four.astype(jnp.float32) * outputs, axis=-1)
    deltas = jnp.transpose(deltas, (1, 2, 0))[..., None]
    grad_prob = jnp.einsum("bhgd,whd->hgbw", g_four, v_three, preferred_element_type=jnp.float32)
    grad_score = (prob_rows * (grad_prob - deltas)).astype(jnp.bfloat16)
    grad_query = (
        jnp.einsum("hgbw,whd->bhgd", grad_score, k_three, preferred_element_type=jnp.float32)
        * score_scale
    ).astype(jnp.bfloat16)
    grad_key = (
        jnp.einsum("hgbw,bhgd->whd", grad_score, q_four, preferred_element_type=jnp.float32)
        * score_scale
    )
    grad_value = jnp.einsum("hgbw,bhgd->whd", prob_half, g_four, preferred_element_type=jnp.float32)
    return (grad_query.reshape(query_rows, -1), grad_key, grad_value)


def projection_term(full_rows, grad_part):
    return lax.dot_general(
        full_rows, grad_part, (((0,), (0,)), ((), ())), preferred_element_type=jnp.float32
    )


def body(
    queries_first,
    queries_second,
    grads_first,
    grads_second,
    key_states,
    value_states,
    doc_lengths,
    hidden_states,
):
    tok_rows = key_states.shape[0]
    kv_width = key_states.shape[1]
    window = (REACH + 1) * tok_rows
    here = lax.axis_index("tok")
    stacked = jnp.concatenate([key_states, value_states], axis=1)
    blocks = [stacked]
    current = stacked
    for hop_count in range(REACH):
        current = passed_along(current, "tok", 1)
        blocks.append(current)
    window_rows = jnp.concatenate(blocks[::-1], axis=0)
    key_window = window_rows[:, :kv_width]
    value_window = window_rows[:, kv_width:]
    doc_ends = jnp.cumsum(doc_lengths)
    query_places = here * tok_rows + jnp.arange(tok_rows, dtype=jnp.int32)
    key_places = (here - REACH) * tok_rows + jnp.arange(window, dtype=jnp.int32)
    allowed = causal_mask(query_places, key_places, doc_ends)
    first_q, first_k, first_v = attend_grads(
        queries_first, grads_first, key_window, value_window, allowed
    )
    second_q, second_k, second_v = attend_grads(
        queries_second, grads_second, key_window, value_window, allowed
    )
    window_grads = jnp.stack([first_k + second_k, first_v + second_v], axis=2).reshape(window, -1)

    def block_term(back_steps):
        return window_grads[(REACH - back_steps) * tok_rows : (REACH - back_steps + 1) * tok_rows]

    running = block_term(0)
    for back_steps in range(1, REACH + 1):
        running = running + passed_along(
            block_term(back_steps).astype(jnp.bfloat16), "tok", -back_steps
        ).astype(jnp.float32)
    kv_grads = running.astype(jnp.bfloat16)
    full_rows = lax.all_gather(hidden_states, "head", axis=1, tiled=True)
    weight_grad = lax.psum_scatter(
        projection_term(full_rows, kv_grads), "tok", scatter_dimension=0, tiled=True
    )
    return (first_q, second_q, weight_grad)


def solution(mesh):
    placed = (
        P("tok", "head"),
        P("tok", "head"),
        P("tok", "head"),
        P("tok", "head"),
        P("tok", "head"),
        P("tok", "head"),
        P(),
        P("tok", "head"),
    )
    return jax.shard_map(
        body,
        mesh=mesh,
        in_specs=placed,
        out_specs=(P("tok", "head"), P("tok", "head"), P("tok", "head")),
        check_vma=False,
    )
```

profile of v0, /device:TPU:0, one launch (start us, length us, event | category | flops | bytes accessed | tf_op | source)
XLA Modules:
  0.0 226.2 jit_solution(16287980497966648228)
XLA Ops:
  9.3 4.9 %collective-permute-start = (bf16[256,512]{0,1:T(8,128)(2,1)S(1)}, bf16[256,512]{0,1:T(8,128)(2,1)S(1)}, u32[]{:S(2)}, u32[]{:S(2)}) collective-permute-start(bf16[256,512]{0,1:T(8,128)(2,1)S(1)} %pad_maximum_fusion.1), channel_id=1, source_target_pairs={{0,4},{4,8},{8,12},{12,16},{16,20},{20,24},{24,28},{1,5},{5,9},{9,... | collective-permute-start | bytes 786440 | tf_op jit(solution)/shard_map/ppermute | solution.py:15
  14.3 5.4 %collective-permute-done = bf16[256,512]{0,1:T(8,128)(2,1)S(1)} collective-permute-done((bf16[256,512]{0,1:T(8,128)(2,1)S(1)}, bf16[256,512]{0,1:T(8,128)(2,1)S(1)}, u32[]{:S(2)}, u32[]{:S(2)}) %collective-permute-start) | collective-permute-done | bytes 262176 | tf_op jit(solution)/shard_map/ppermute | solution.py:15
  19.7 4.4 %collective-permute-start.1 = (bf16[256,512]{0,1:T(8,128)(2,1)S(1)}, bf16[256,512]{0,1:T(8,128)(2,1)S(1)}, u32[]{:S(2)}, u32[]{:S(2)}) collective-permute-start(bf16[256,512]{0,1:T(8,128)(2,1)S(1)} %collective-permute-done), channel_id=1, source_target_pairs={{0,4},{4,8},{8,12},{12,16},{16,20},{20,24},{24,28},{1,5},{5,9},{9,... | collective-permute-start | bytes 786440 | tf_op jit(solution)/shard_map/ppermute | solution.py:15
  25.1 3.6 %collective-permute-done.1 = bf16[256,512]{0,1:T(8,128)(2,1)S(1)} collective-permute-done((bf16[256,512]{0,1:T(8,128)(2,1)S(1)}, bf16[256,512]{0,1:T(8,128)(2,1)S(1)}, u32[]{:S(2)}, u32[]{:S(2)}) %collective-permute-start.1) | collective-permute-done | bytes 262176 | tf_op jit(solution)/shard_map/ppermute | solution.py:15
  28.8 4.4 %collective-permute-start.2 = (bf16[256,512]{0,1:T(8,128)(2,1)S(1)}, bf16[256,512]{0,1:T(8,128)(2,1)S(1)}, u32[]{:S(2)}, u32[]{:S(2)}) collective-permute-start(bf16[256,512]{0,1:T(8,128)(2,1)S(1)} %collective-permute-done.1), channel_id=1, source_target_pairs={{0,4},{4,8},{8,12},{12,16},{16,20},{20,24},{24,28},{1,5},{5,9},{9,... | collective-permute-start | bytes 786440 | tf_op jit(solution)/shard_map/ppermute | solution.py:15
  33.2 1.9 copy.65
  35.1 1.2 copy.73
  38.6 4.9 %fusion.45 = (f32[2,3,256]{2,1,0:T(4,128)S(1)}, f32[2,3,256,1024]{2,3,1,0:T(8,128)}) fusion(pred[256,1024]{0,1:T(8,128)(4,1)S(1)} %and_and_fusion, bf16[1024,2,128,1]{0,2,3,1:T(8,128)(2,1)S(1)} %bitcast.155, bf16[256,2,3,128]{0,3,2,1:T(8,128)(2,1)S(1)} %bitcast.169), kind=kOutput, calls=%fused_computation.71 | convolution fusion | flops 408945664 | bytes 7477248 | tf_op jit(solution)/shard_map/sub | solution.py:46
  43.5 3.3 %fusion.15 = bf16[2,3,256,1024]{2,3,1,0:T(8,128)(2,1)S(1)} fusion(f32[2,3,256,1024]{2,3,1,0:T(8,128)} %get-tuple-element.20, f32[2,3,256]{2,1,0:T(4,128)S(1)} %get-tuple-element.19), kind=kLoop, calls=%fused_computation.24 | loop fusion | flops 3145728 | bytes 9443328 | tf_op jit(solution)/shard_map/convert_element_type | solution.py:48
  46.8 2.1 convolution_bitcast_fusion.1
  50.0 2.1 fusion.3
  52.1 6.2 %fusion.44 = (f32[2,3,256]{2,1,0:T(4,128)S(1)}, f32[2,3,256,1024]{2,3,1,0:T(8,128)}) fusion(pred[256,1024]{0,1:T(8,128)(4,1)} %copy-done.12, bf16[1024,2,128,1]{0,2,3,1:T(8,128)(2,1)} %bitcast.156, bf16[256,2,3,128]{0,3,2,1:T(8,128)(2,1)} %bitcast.171), kind=kOutput, calls=%fused_computation.70 | convolution fusion | flops 408945664 | bytes 7477248 | tf_op jit(solution)/shard_map/sub | solution.py:46
  58.2 3.4 %fusion.14 = bf16[2,3,256,1024]{2,3,1,0:T(8,128)(2,1)S(1)} fusion(f32[2,3,256,1024]{2,3,1,0:T(8,128)} %get-tuple-element.18, f32[2,3,256]{2,1,0:T(4,128)S(1)} %get-tuple-element.17), kind=kLoop, calls=%fused_computation.23 | loop fusion | flops 3145728 | bytes 9443328 | tf_op jit(solution)/shard_map/convert_element_type | solution.py:48
  62.8 1.1 fusion.21
  68.3 1.5 collective-permute-start.4
  69.7 1.3 collective-permute-start.5
  71.0 1.3 collective-permute-start.3
  72.4 11.4 %collective-permute-done.4 = bf16[256,512]{0,1:T(8,128)(2,1)S(1)} collective-permute-done((bf16[256,512]{0,1:T(8,128)(2,1)S(1)}, bf16[256,512]{0,1:T(8,128)(2,1)S(1)}, u32[]{:S(2)}, u32[]{:S(2)}) %collective-permute-start.4) | collective-permute-done | bytes 262176 | tf_op jit(solution)/shard_map/ppermute | solution.py:15
  84.6 1.5 collective-permute-done.3
  86.3 5.0 %convolution_bitcast_fusion = f32[3072,512]{0,1:T(8,128)} fusion(bf16[256,512]{0,1:T(8,128)(2,1)S(1)} %fusion.35, bf16[256,3072]{1,0:T(8,128)(2,1)} %all-gather.2.cloned.1.call-done), kind=kOutput, calls=%fused_computation.12 | convolution fusion | flops 805306368 | bytes 8126464 | tf_op jit(solution)/shard_map/dot_general | solution.py:67
  91.4 1.6 fusion.25
  93.9 2.7 %fusion.24 = bf16[2,128,3,256]{3,1,2,0:T(8,128)(2,1)S(1)} fusion(bf16[1024,2,128,1]{0,2,3,1:T(8,128)(2,1)} %bitcast.158, bf16[2,3,256,1024]{2,3,1,0:T(8,128)(2,1)} %copy-done), kind=kOutput, calls=%fused_computation.44 | convolution fusion | flops 403046400 | bytes 4063232 | tf_op jit(solution)/shard_map/hgbw,whd->bhgd/dot_general | solution.py:55
  97.5 119.5 %reduce-scatter.2.cloned.1.call-done = f32[384,512]{0,1:T(8,128)} async-done(((f32[3072,512]{0,1:T(8,128)}), f32[384,512]{0,1:T(8,128)}) %reduce-scatter.2.cloned.1.call-update) | async-done | bytes 786448 | tf_op jit(solution)/shard_map/reduce_scatter | solution.py:117
  217.1 2.3 %copy.91 = f32[384,512]{1,0:T(8,128)} copy(f32[384,512]{0,1:T(8,128)} %reduce-scatter.2.cloned.1.call-done) | data formatting | bytes 1572864
  (67 shorter events, 14.7 us)
Async XLA Ops:
  7.2 29.1 %copy-start.10 = (bf16[256,768]{1,0:T(8,128)(2,1)S(1)}, bf16[256,768]{1,0:T(8,128)(2,1)}, u32[]{:S(2)}) copy-start(bf16[256,768]{1,0:T(8,128)(2,1)} %param.10) | copy-start | bytes 1179652
  7.2 30.1 %copy-start.11 = (bf16[256,768]{1,0:T(8,128)(2,1)S(1)}, bf16[256,768]{1,0:T(8,128)(2,1)}, u32[]{:S(2)}) copy-start(bf16[256,768]{1,0:T(8,128)(2,1)} %param.11) | copy-start | bytes 1179652
  7.2 79.1 %all-gather.2.cloned.1.call-start = ((), (), s32[]{:S(2)}) async-start(), calls=%async_computation.1 | async-start | bytes 1966080 | tf_op jit(solution)/shard_map/all_gather | solution.py:116
  9.3 10.4 %collective-permute-start = (bf16[256,512]{0,1:T(8,128)(2,1)S(1)}, bf16[256,512]{0,1:T(8,128)(2,1)S(1)}, u32[]{:S(2)}, u32[]{:S(2)}) collective-permute-start(bf16[256,512]{0,1:T(8,128)(2,1)S(1)} %pad_maximum_fusion.1), channel_id=1, source_target_pairs={{0,4},{4,8},{8,12},{12,16},{16,20},{20,24},{24,28},{1,5},{5,9},{9,... | collective-permute-start | bytes 786440 | tf_op jit(solution)/shard_map/ppermute | solution.py:15
  14.2 202.8 %reduce-scatter.2.cloned.1.call-start = ((), (), s32[]{:S(2)}) async-start(), calls=%async_computation.2 | async-start | bytes 7077888 | tf_op jit(solution)/shard_map/reduce_scatter | solution.py:117
  19.7 9.1 %collective-permute-start.1 = (bf16[256,512]{0,1:T(8,128)(2,1)S(1)}, bf16[256,512]{0,1:T(8,128)(2,1)S(1)}, u32[]{:S(2)}, u32[]{:S(2)}) collective-permute-start(bf16[256,512]{0,1:T(8,128)(2,1)S(1)} %collective-permute-done), channel_id=1, source_target_pairs={{0,4},{4,8},{8,12},{12,16},{16,20},{20,24},{24,28},{1,5},{5,9},{9,... | collective-permute-start | bytes 786440 | tf_op jit(solution)/shard_map/ppermute | solution.py:15
  28.8 9.6 %collective-permute-start.2 = (bf16[256,512]{0,1:T(8,128)(2,1)S(1)}, bf16[256,512]{0,1:T(8,128)(2,1)S(1)}, u32[]{:S(2)}, u32[]{:S(2)}) collective-permute-start(bf16[256,512]{0,1:T(8,128)(2,1)S(1)} %collective-permute-done.1), channel_id=1, source_target_pairs={{0,4},{4,8},{8,12},{12,16},{16,20},{20,24},{24,28},{1,5},{5,9},{9,... | collective-permute-start | bytes 786440 | tf_op jit(solution)/shard_map/ppermute | solution.py:15
  36.3 7.2 %copy-start.7 = (bf16[256,768]{0,1:T(8,128)(2,1)}, bf16[256,768]{0,1:T(8,128)(2,1)S(1)}, u32[]{:S(2)}) copy-start(bf16[256,768]{0,1:T(8,128)(2,1)S(1)} %copy.73) | copy-start | bytes 1179652
  38.3 5.2 %copy-start.12 = (pred[256,1024]{0,1:T(8,128)(4,1)}, pred[256,1024]{0,1:T(8,128)(4,1)S(1)}, u32[]{:S(2)}) copy-start(pred[256,1024]{0,1:T(8,128)(4,1)S(1)} %and_and_fusion) | copy-start | bytes 786436
  38.6 5.0 %copy-start.2 = (bf16[1024,256]{0,1:T(8,128)(2,1)}, bf16[1024,256]{0,1:T(8,128)(2,1)S(1)}, u32[]{:S(2)}) copy-start(bf16[1024,256]{0,1:T(8,128)(2,1)S(1)} %get-tuple-element.16) | copy-start | bytes 1572868
  38.6 10.4 %copy-start.3 = (bf16[1024,256]{0,1:T(8,128)(2,1)}, bf16[1024,256]{0,1:T(8,128)(2,1)S(1)}, u32[]{:S(2)}) copy-start(bf16[1024,256]{0,1:T(8,128)(2,1)S(1)} %get-tuple-element.15) | copy-start | bytes 1572868
  46.8 3.2 %copy-start.1 = (f32[2,3,256,1024]{2,3,1,0:T(8,128)S(1)}, f32[2,3,256,1024]{2,3,1,0:T(8,128)}, u32[]{:S(2)}) copy-start(f32[2,3,256,1024]{2,3,1,0:T(8,128)} %get-tuple-element.20) | copy-start | bytes 18874372
  58.2 3.4 %copy-start.4 = (bf16[1024,256]{0,1:T(8,128)(2,1)S(1)}, bf16[1024,256]{0,1:T(8,128)(2,1)}, u32[]{:S(2)}) copy-start(bf16[1024,256]{0,1:T(8,128)(2,1)} %copy-done.3) | copy-start | bytes 1572868
  58.2 3.4 %copy-start.6 = (bf16[256,768]{0,1:T(8,128)(2,1)S(1)}, bf16[256,768]{0,1:T(8,128)(2,1)}, u32[]{:S(2)}) copy-start(bf16[256,768]{0,1:T(8,128)(2,1)} %copy.68) | copy-start | bytes 1179652
  61.6 1.2 copy-start.5
  61.6 3.7 %slice-start = ((s8[6291456]{0:T(1024)(128)(4,1)}), s8[4194304]{0:T(1024)(128)(4,1)S(1)}, s32[]{:S(2)}) async-start(s8[6291456]{0:T(1024)(128)(4,1)} %bitcast.153), calls=%async_computation.3 | async-start | bytes 8388608
  62.8 1.3 copy-start.8
  62.8 2.5 %slice-start.1 = ((s8[6291456]{0:T(1024)(128)(4,1)}), s8[2097152]{0:T(1024)(128)(4,1)S(1)}, s32[]{:S(2)}) async-start(s8[6291456]{0:T(1024)(128)(4,1)} %bitcast.153), calls=%async_computation.4 | async-start | bytes 4194304
  65.3 1.1 copy-start.9
  66.4 1.7 copy-start
  68.3 15.5 %collective-permute-start.4 = (bf16[256,512]{0,1:T(8,128)(2,1)S(1)}, bf16[256,512]{0,1:T(8,128)(2,1)S(1)}, u32[]{:S(2)}, u32[]{:S(2)}) collective-permute-start(bf16[256,512]{0,1:T(8,128)(2,1)S(1)} %bitcast.177), channel_id=1, source_target_pairs={{8,0},{12,4},{16,8},{20,12},{24,16},{28,20},{9,1},{13,5},{17,9},{2... | collective-permute-start | bytes 786440 | tf_op jit(solution)/shard_map/ppermute | solution.py:15
  69.7 14.9 %collective-permute-start.5 = (bf16[256,512]{0,1:T(8,128)(2,1)S(1)}, bf16[256,512]{0,1:T(8,128)(2,1)S(1)}, u32[]{:S(2)}, u32[]{:S(2)}) collective-permute-start(bf16[256,512]{0,1:T(8,128)(2,1)S(1)} %bitcast.176), channel_id=1, source_target_pairs={{12,0},{16,4},{20,8},{24,12},{28,16},{13,1},{17,5},{21,9},{25,13},... | collective-permute-start | bytes 786440 | tf_op jit(solution)/shard_map/ppermute | solution.py:15
  71.0 15.1 %collective-permute-start.3 = (bf16[256,512]{0,1:T(8,128)(2,1)S(1)}, bf16[256,512]{0,1:T(8,128)(2,1)S(1)}, u32[]{:S(2)}, u32[]{:S(2)}) collective-permute-start(bf16[256,512]{0,1:T(8,128)(2,1)S(1)} %bitcast.175), channel_id=1, source_target_pairs={{4,0},{8,4},{12,8},{16,12},{20,16},{24,20},{28,24},{5,1},{9,5},{13... | collective-permute-start | bytes 786440 | tf_op jit(solution)/shard_map/ppermute | solution.py:15
Sparse Core Ops, SparseCore 0:
  14.4 19.9 all-gather.1
  91.5 125.5 reduce-scatter.1
where the time goes:
time: 227 us; the launch traced here: 226 us
  waiting for transfers between devices  142 us (63%)
  matrix products  30.4 us (13%)
  starting transfers between devices  17.8 us (8%)
  between operations  14.5 us (6%)
  local copies, waits for them, and re-layouts  12.1 us (5%)
  other arithmetic  9.09 us (4%)
    reduce_scatter x1, waiting for transfers between devices, body(): lax.psum_scatter(projection_term(full_rows, kv_grads), 'tok', scatter_dim...  120 us
    ppermute x6, waiting for transfers between devices, passed_along(): lax.ppermute(value, axis, [(source, source + steps) for source in range(i...  22.8 us
    ppermute x6, starting transfers between devices, passed_along(): lax.ppermute(value, axis, [(source, source + steps) for source in range(i...  17.7 us
    unnamed x39, local copies, waits for them, and re-layouts  11.9 us
    sub x2, matrix products, attend_grads(): raised = jnp.exp(scores - row_max)  11.1 us
    convert_element_type x2, other arithmetic, attend_grads(): prob_half = prob_rows.astype(jnp.bfloat16)  6.66 us
    dot_general x1, matrix products, projection_term(): lax.dot_general(full_rows, grad_part, (((0,), (0,)), ((), ())), preferred...  5.05 us
  transfers between devices with their start and end apart: 8, of which 6 were waited for; matrix products, arithmetic and copies ran while one was open for 18% of the time, Pallas kernels for 0%

commit v1 on v0

v1 whole, which is shorter than its diff:
```python
import functools
import math

import jax
import jax.numpy as jnp
from jax import lax
from jax.experimental import pallas as pl
from jax.experimental.pallas import tpu as pltpu
from jax.sharding import PartitionSpec as P

HD = 128
REACH = 3
NT = (((1,), (1,)), ((), ()))


def attend_kernel(rows, group, here_ref, lens_ref, q1_ref, q2_ref, g1_ref, g2_ref, b3_ref, b2_ref, b1_ref, b0_ref,
                  dq1_ref, dq2_ref, f3_ref, f2_ref, f1_ref, own_ref, kv_ref, kt_ref, bias_ref, acc_ref):
    window = (REACH + 1) * rows
    half = rows // 2
    span = window - half
    scale = 1.0 / math.sqrt(HD)
    for i, ref in enumerate((b3_ref, b2_ref, b1_ref, b0_ref)):
        kv_ref[i * rows:(i + 1) * rows, :] = ref[...]
    kt_ref[...] = kv_ref[:, :HD].T
    base = here_ref[0] * rows
    places = base + lax.broadcasted_iota(jnp.int32, (1, rows), 1)

    def later(i, carry):
        end, first = carry
        end = end + lens_ref[i]
        return end, jnp.where(places >= end, end, first)

    _, first = lax.fori_loop(0, lens_ref.shape[0], later, (jnp.int32(0), jnp.zeros((1, rows), jnp.int32)))
    for side in range(2):
        keys = base - REACH * rows + side * half + lax.broadcasted_iota(jnp.int32, (span, half), 0)
        own = slice(side * half, (side + 1) * half)
        allowed = (keys >= first[:, own]) & (keys <= places[:, own])
        bias_ref[side] = jnp.where(allowed, 0.0, -1e30)
    acc_ref[...] = jnp.zeros_like(acc_ref)
    units = [(l, j) for l in range(2) for j in range(group)]
    for side in range(2):
        r = slice(side * half, (side + 1) * half)
        w = slice(side * half, side * half + span)
        k, v, kt = kv_ref[w, :HD], kv_ref[w, HD:], kt_ref[:, w]
        bias = bias_ref[side]
        bias2 = jnp.concatenate([bias, bias], axis=1)
        for n in range(0, len(units), 2):
            pair = units[n:n + 2]
            q = jnp.concatenate([(q1_ref, q2_ref)[l][r, j * HD:(j + 1) * HD] for l, j in pair], axis=0)
            g = jnp.concatenate([(g1_ref, g2_ref)[l][r, j * HD:(j + 1) * HD] for l, j in pair], axis=0)
            s = lax.dot_general(k, q, NT, preferred_element_type=jnp.float32) * (scale * math.log2(math.e)) + bias2
            dp = lax.dot_general(v, g, NT, preferred_element_type=jnp.float32)
            raised = jnp.exp2(s - jnp.max(s, axis=0, keepdims=True))
            p = raised * (1.0 / jnp.sum(raised, axis=0, keepdims=True))
            ph = p.astype(jnp.bfloat16)
            delta = jnp.sum(ph.astype(jnp.float32) * dp, axis=0, keepdims=True)
            ds = (p * (dp - delta)).astype(jnp.bfloat16)
            acc_ref[w, HD:] += jnp.dot(ph, g, preferred_element_type=jnp.float32)
            acc_ref[w, :HD] += jnp.dot(ds, q, preferred_element_type=jnp.float32)
            dqt = jnp.dot(kt, ds, preferred_element_type=jnp.float32) * scale
            dq = dqt.T.astype(jnp.bfloat16)
            for i, (l, j) in enumerate(pair):
                (dq1_ref, dq2_ref)[l][r, j * HD:(j + 1) * HD] = dq[i * half:(i + 1) * half]
    for i, ref in enumerate((f3_ref, f2_ref, f1_ref)):
        block = slice(i * rows, (i + 1) * rows)
        ref[:, :HD] = (acc_ref[block, :HD] * scale).astype(jnp.bfloat16)
        ref[:, HD:] = acc_ref[block, HD:].astype(jnp.bfloat16)
    own_ref[:, :HD] = acc_ref[REACH * rows:, :HD] * scale
    own_ref[:, HD:] = acc_ref[REACH * rows:, HD:]


def attend(c, kv_heads, here, lens, q1, q2, g1, g2, blocks):
    rows, width = q1.shape
    group = width // (kv_heads * HD)
    window = (REACH + 1) * rows
    cols = pl.BlockSpec((rows, group * HD), lambda i: (0, c))
    whole = lambda a: pl.BlockSpec(a.shape, lambda i: (0,) * a.ndim)
    smem = pl.BlockSpec(memory_space=pltpu.SMEM)
    flops = 5 * 2 * 2 * group * rows * window * HD
    return pl.pallas_call(
        functools.partial(attend_kernel, rows, group),
        grid=(1,),
        in_specs=[smem, smem, cols, cols, cols, cols] + [whole(b) for b in blocks],
        out_specs=[pl.BlockSpec((rows, group * HD), lambda i: (0, 0))] * 2
        + [pl.BlockSpec((rows, 2 * HD), lambda i: (0, 0))] * (REACH + 1),
        out_shape=[jax.ShapeDtypeStruct((rows, group * HD), jnp.bfloat16)] * 2
        + [jax.ShapeDtypeStruct((rows, 2 * HD), jnp.bfloat16)] * REACH + [jax.ShapeDtypeStruct((rows, 2 * HD), jnp.float32)],
        scratch_shapes=[pltpu.VMEM((window, 2 * HD), jnp.bfloat16), pltpu.VMEM((HD, window), jnp.bfloat16),
                        pltpu.VMEM((2, window - rows // 2, rows // 2), jnp.float32), pltpu.VMEM((window, 2 * HD), jnp.float32)],
        compiler_params=pltpu.CompilerParams(vmem_limit_bytes=48 * 1024 * 1024),
        cost_estimate=pl.CostEstimate(flops=flops, bytes_accessed=3 << 20, transcendentals=2 * group * rows * window),
        name="attend",
    )(here, lens, q1, q2, g1, g2, *blocks)


def moved(value, axis, place):
    pairs = [(i, place(i)) for i in range(lax.axis_size(axis))]
    return lax.ppermute(value, axis, [(i, j) for i, j in pairs if j is not None])


def project_kernel(picks_ref, hid_ref, *refs):
    blocks, (own_ref, away_ref) = refs[:-2], refs[-2:]
    total = None
    for j, block in enumerate(blocks):
        term = jnp.dot(hid_ref[picks_ref[j]], block[...], preferred_element_type=jnp.float32)
        total = term if total is None else total + term
    lanes, part = away_ref.shape[0] + 1, own_ref.shape[0]
    mine = picks_ref[len(blocks)]
    refs[-2][...] = jnp.zeros_like(own_ref)
    for d in range(lanes):
        piece = total[d * part:(d + 1) * part]

        @pl.when(mine == d)
        def _():
            own_ref[...] = piece

        for e in range(1, lanes):
            @pl.when((mine ^ e) == d)
            def _():
                away_ref[e - 1] = piece.astype(jnp.bfloat16)


def project(picks, hid, blocks, lanes):
    count, width, rows = hid.shape
    part = width // lanes
    columns = blocks[0].shape[1]
    vmem = pl.BlockSpec(memory_space=pltpu.VMEM)
    return pl.pallas_call(
        project_kernel,
        in_specs=[pl.BlockSpec(memory_space=pltpu.SMEM)] + [vmem] * (1 + count),
        out_specs=[vmem, vmem],
        out_shape=[jax.ShapeDtypeStruct((part, columns), jnp.float32),
                   jax.ShapeDtypeStruct((lanes - 1, part, columns), jnp.bfloat16)],
        compiler_params=pltpu.CompilerParams(vmem_limit_bytes=32 * 1024 * 1024),
        cost_estimate=pl.CostEstimate(flops=2 * count * width * rows * columns, bytes_accessed=4 << 20, transcendentals=0),
        name="project",
    )(picks, hid, *blocks)


def body(queries_first, queries_second, grads_first, grads_second, key_states, value_states, doc_lengths, hidden_states):
    rows = key_states.shape[0]
    kv_heads = key_states.shape[1] // HD
    tokens, heads = lax.axis_size("tok"), lax.axis_size("head")
    lanes = tokens // heads
    here, head = lax.axis_index("tok"), lax.axis_index("head")
    line, lane = here // lanes, here % lanes
    place = here.reshape(1).astype(jnp.int32)

    windows = []
    for c in range(kv_heads):
        own = jnp.concatenate([key_states[:, c * HD:(c + 1) * HD], value_states[:, c * HD:(c + 1) * HD]], axis=1)
        windows.append([moved(own, "tok", lambda t, s=s: t + s if t + s < tokens else None) for s in range(REACH, 0, -1)] + [own])

    def crossed(i):
        t, h = i // heads, i % heads
        return (h * lanes + t % lanes) * heads + t // lanes

    hid = moved(hidden_states.T[None], ("tok", "head"), crossed)
    step = heads // 2
    while step:
        hid = jnp.concatenate([hid, moved(hid, "head", lambda h: h ^ step)], axis=0)
        step //= 2
    order = [0]
    step = heads // 2
    while step:
        order = order + [i ^ step for i in order]
        step //= 2
    slot_of = jnp.asarray([order.index(i) for i in range(heads)], jnp.int32)
    picks = jnp.concatenate([slot_of[line ^ head ^ jnp.arange(heads)], lane.reshape(1)]).astype(jnp.int32)

    firsts, seconds, parts = [], [], []
    for c in range(kv_heads):
        first, second, *far, own = attend(
            c, kv_heads, place, doc_lengths, queries_first, queries_second, grads_first, grads_second, windows[c])
        firsts.append(first)
        seconds.append(second)
        total = own
        for s in range(1, REACH + 1):
            back = moved(far[REACH - s], "tok", lambda t, s=s: t - s if t >= s else None)
            total = total + back.astype(jnp.float32)
        kv_grads = total.astype(jnp.bfloat16)
        blocks = [kv_grads] + [
            moved(kv_grads, "tok", lambda t, j=j: ((t // lanes) ^ j) * lanes + t % lanes) for j in range(1, heads)]
        mine, away = project(picks, hid, blocks, lanes)
        for d in range(1, lanes):
            mine = mine + moved(away[d - 1], "tok", lambda t, d=d: t ^ d).astype(jnp.float32)
        parts.append(mine)
    return (jnp.concatenate(firsts, axis=1), jnp.concatenate(seconds, axis=1), jnp.concatenate(parts, axis=1))


def solution(mesh):
    split = P("tok", "head")
    return jax.shard_map(
        body,
        mesh=mesh,
        in_specs=(split,) * 6 + (P(), split),
        out_specs=(split,) * 3,
        check_vma=False,
    )
```

time: 227 us -> 109 us (0.48)
  the two profiles are of different devices: /device:TPU:0 before, /device:TPU:12 now
where the time goes in v1:
time: 109 us
  starting transfers between devices  46.1 us (42%)
  waiting for transfers between devices  39.2 us (36%)
  Pallas kernels  16.4 us (15%)
  local copies, waits for them, and re-layouts  3.01 us (3%)
  other arithmetic  2.96 us (3%)
  between operations  1.1 us (1%)
    ppermute x23, starting transfers between devices, moved(): lax.ppermute(value, axis, [(i, j) for i, j in pairs if j is not None])  46.1 us
    ppermute x23, waiting for transfers between devices, moved(): lax.ppermute(value, axis, [(i, j) for i, j in pairs if j is not None])  39.2 us
    pallas_call x2, Pallas kernels, attend(): pl.pallas_call(functools.partial(attend_kernel, rows, group), grid=(1,),...  14.1 us
    pallas_call x2, Pallas kernels, project(): pl.pallas_call(project_kernel, in_specs=[pl.BlockSpec(memory_space=pltpu....  2.31 us
  transfers between devices with their start and end apart: 23, of which 11 were waited for; matrix products, arithmetic and copies ran while one was open for 3% of the time, Pallas kernels for 15%

profile of v1, /device:TPU:12, one launch (start us, length us, event | category | flops | bytes accessed | tf_op | source)
XLA Modules:
  0.0 108.9 jit_solution(9951252571328028758)
XLA Ops:
  2.0 2.9 %collective-permute-start.6 = (bf16[1,768,256]{2,1,0:T(8,128)(2,1)S(1)}, bf16[1,768,256]{2,1,0:T(8,128)(2,1)S(1)}, u32[]{:S(2)}, u32[]{:S(2)}) collective-permute-start(bf16[1,768,256]{2,1,0:T(8,128)(2,1)S(1)} %bitcast.11), channel_id=1, source_target_pairs={{0,0},{1,8},{2,16},{3,24},{4,4},{5,12},{6,20},{7,28},{8,1},{9,9},{... | collective-permute-start | bytes 1179656 | tf_op jit(solution)/shard_map/ppermute | solution.py:98
  5.8 2.2 %collective-permute-start = (bf16[256,256]{1,0:T(8,128)(2,1)S(1)}, bf16[256,256]{1,0:T(8,128)(2,1)S(1)}, u32[]{:S(2)}, u32[]{:S(2)}) collective-permute-start(bf16[256,256]{1,0:T(8,128)(2,1)S(1)} %pad_maximum_fusion.4.b0_ref), channel_id=1, source_target_pairs={{0,12},{4,16},{8,20},{12,24},{16,28},{1,13},{5,17},{9,21},{13,25},... | collective-permute-start | bytes 393224 | tf_op jit(solution)/shard_map/ppermute | solution.py:98
  8.1 4.7 %collective-permute-start.1 = (bf16[256,256]{1,0:T(8,128)(2,1)S(1)}, bf16[256,256]{1,0:T(8,128)(2,1)S(1)}, u32[]{:S(2)}, u32[]{:S(2)}) collective-permute-start(bf16[256,256]{1,0:T(8,128)(2,1)S(1)} %pad_maximum_fusion.4.b0_ref), channel_id=1, source_target_pairs={{0,8},{4,12},{8,16},{12,20},{16,24},{20,28},{1,9},{5,13},{9,17},{1... | collective-permute-start | bytes 393224 | tf_op jit(solution)/shard_map/ppermute | solution.py:98
  12.8 1.9 %collective-permute-start.2 = (bf16[256,256]{1,0:T(8,128)(2,1)S(1)}, bf16[256,256]{1,0:T(8,128)(2,1)S(1)}, u32[]{:S(2)}, u32[]{:S(2)}) collective-permute-start(bf16[256,256]{1,0:T(8,128)(2,1)S(1)} %pad_maximum_fusion.4.b0_ref), channel_id=1, source_target_pairs={{0,4},{4,8},{8,12},{12,16},{16,20},{20,24},{24,28},{1,5},{5,9},{9,... | collective-permute-start | bytes 393224 | tf_op jit(solution)/shard_map/ppermute | solution.py:98
  14.8 1.3 %collective-permute-start.3 = (bf16[256,256]{1,0:T(8,128)(2,1)S(1)}, bf16[256,256]{1,0:T(8,128)(2,1)S(1)}, u32[]{:S(2)}, u32[]{:S(2)}) collective-permute-start(bf16[256,256]{1,0:T(8,128)(2,1)S(1)} %pad_maximum_fusion.5.b0_ref), channel_id=1, source_target_pairs={{0,12},{4,16},{8,20},{12,24},{16,28},{1,13},{5,17},{9,21},{13,25},... | collective-permute-start | bytes 393224 | tf_op jit(solution)/shard_map/ppermute | solution.py:98
  16.1 8.2 %collective-permute-done.6 = bf16[1,768,256]{2,1,0:T(8,128)(2,1)S(1)} collective-permute-done((bf16[1,768,256]{2,1,0:T(8,128)(2,1)S(1)}, bf16[1,768,256]{2,1,0:T(8,128)(2,1)S(1)}, u32[]{:S(2)}, u32[]{:S(2)}) %collective-permute-start.6) | collective-permute-done | bytes 393248 | tf_op jit(solution)/shard_map/ppermute | solution.py:98
  25.2 2.1 %collective-permute-start.4 = (bf16[256,256]{1,0:T(8,128)(2,1)S(1)}, bf16[256,256]{1,0:T(8,128)(2,1)S(1)}, u32[]{:S(2)}, u32[]{:S(2)}) collective-permute-start(bf16[256,256]{1,0:T(8,128)(2,1)S(1)} %pad_maximum_fusion.5.b0_ref), channel_id=1, source_target_pairs={{0,8},{4,12},{8,16},{12,20},{16,24},{20,28},{1,9},{5,13},{9,17},{1... | collective-permute-start | bytes 393224 | tf_op jit(solution)/shard_map/ppermute | solution.py:98
  28.0 9.0 %collective-permute-start.5 = (bf16[256,256]{1,0:T(8,128)(2,1)S(1)}, bf16[256,256]{1,0:T(8,128)(2,1)S(1)}, u32[]{:S(2)}, u32[]{:S(2)}) collective-permute-start(bf16[256,256]{1,0:T(8,128)(2,1)S(1)} %pad_maximum_fusion.5.b0_ref), channel_id=1, source_target_pairs={{0,4},{4,8},{8,12},{12,16},{16,20},{20,24},{24,28},{1,5},{5,9},{9,... | collective-permute-start | bytes 393224 | tf_op jit(solution)/shard_map/ppermute | solution.py:98
  37.1 7.1 %attend.2 = (bf16[256,384]{1,0:T(8,128)(2,1)S(1)}, bf16[256,384]{1,0:T(8,128)(2,1)S(1)}, bf16[256,256]{1,0:T(8,128)(2,1)S(1)}, bf16[256,256]{1,0:T(8,128)(2,1)S(...) custom-call(s32[1]{0:T(128)} %bitcast.here_ref, s32[8]{0:T(128)S(1)} %copy-done.4, ...), custom_call_target="tpu_custom_call" | custom-call | flops 2013265920 | bytes 3145728 | tf_op jit(solution)/shard_map/attend/pallas_call | solution.py:80
  44.2 3.1 %collective-permute-start.10 = (bf16[256,256]{1,0:T(8,128)(2,1)S(1)}, bf16[256,256]{1,0:T(8,128)(2,1)S(1)}, u32[]{:S(2)}, u32[]{:S(2)}) collective-permute-start(bf16[256,256]{1,0:T(8,128)(2,1)S(1)} %get-tuple-element.25), channel_id=1, source_target_pairs={{8,0},{12,4},{16,8},{20,12},{24,16},{28,20},{9,1},{13,5},{17,9},{2... | collective-permute-start | bytes 393224 | tf_op jit(solution)/shard_map/ppermute | solution.py:98
  47.3 1.3 %collective-permute-start.11 = (bf16[256,256]{1,0:T(8,128)(2,1)S(1)}, bf16[256,256]{1,0:T(8,128)(2,1)S(1)}, u32[]{:S(2)}, u32[]{:S(2)}) collective-permute-start(bf16[256,256]{1,0:T(8,128)(2,1)S(1)} %get-tuple-element.26), channel_id=1, source_target_pairs={{12,0},{16,4},{20,8},{24,12},{28,16},{13,1},{17,5},{21,9},{25,13},... | collective-permute-start | bytes 393224 | tf_op jit(solution)/shard_map/ppermute | solution.py:98
  48.6 2.1 %collective-permute-start.9 = (bf16[256,256]{1,0:T(8,128)(2,1)S(1)}, bf16[256,256]{1,0:T(8,128)(2,1)S(1)}, u32[]{:S(2)}, u32[]{:S(2)}) collective-permute-start(bf16[256,256]{1,0:T(8,128)(2,1)S(1)} %get-tuple-element.24), channel_id=1, source_target_pairs={{4,0},{8,4},{12,8},{16,12},{20,16},{24,20},{28,24},{5,1},{9,5},{13... | collective-permute-start | bytes 393224 | tf_op jit(solution)/shard_map/ppermute | solution.py:98
  50.9 7.1 %attend.3 = (bf16[256,384]{1,0:T(8,128)(2,1)S(1)}, bf16[256,384]{1,0:T(8,128)(2,1)S(1)}, bf16[256,256]{1,0:T(8,128)(2,1)S(1)}, bf16[256,256]{1,0:T(8,128)(2,1)S(...) custom-call(s32[1]{0:T(128)} %bitcast.here_ref, s32[8]{0:T(128)S(1)} %copy-done.4, ...), custom_call_target="tpu_custom_call" | custom-call | flops 2013265920 | bytes 3145728 | tf_op jit(solution)/shard_map/attend/pallas_call | solution.py:80
  57.9 2.7 %collective-permute-start.16 = (bf16[256,256]{1,0:T(8,128)(2,1)S(1)}, bf16[256,256]{1,0:T(8,128)(2,1)S(1)}, u32[]{:S(2)}, u32[]{:S(2)}) collective-permute-start(bf16[256,256]{1,0:T(8,128)(2,1)S(1)} %get-tuple-element.30), channel_id=1, source_target_pairs={{4,0},{8,4},{12,8},{16,12},{20,16},{24,20},{28,24},{5,1},{9,5},{13... | collective-permute-start | bytes 393224 | tf_op jit(solution)/shard_map/ppermute | solution.py:98
  60.7 1.9 %collective-permute-start.17 = (bf16[256,256]{1,0:T(8,128)(2,1)S(1)}, bf16[256,256]{1,0:T(8,128)(2,1)S(1)}, u32[]{:S(2)}, u32[]{:S(2)}) collective-permute-start(bf16[256,256]{1,0:T(8,128)(2,1)S(1)} %get-tuple-element.31), channel_id=1, source_target_pairs={{8,0},{12,4},{16,8},{20,12},{24,16},{28,20},{9,1},{13,5},{17,9},{2... | collective-permute-start | bytes 393224 | tf_op jit(solution)/shard_map/ppermute | solution.py:98
  64.1 3.4 %collective-permute-done.16 = bf16[256,256]{1,0:T(8,128)(2,1)S(1)} collective-permute-done((bf16[256,256]{1,0:T(8,128)(2,1)S(1)}, bf16[256,256]{1,0:T(8,128)(2,1)S(1)}, u32[]{:S(2)}, u32[]{:S(2)}) %collective-permute-start.16) | collective-permute-done | bytes 131104 | tf_op jit(solution)/shard_map/ppermute | solution.py:98
  67.5 4.1 %collective-permute-start.13 = (bf16[256,256]{1,0:T(8,128)(2,1)S(1)}, bf16[256,256]{1,0:T(8,128)(2,1)S(1)}, u32[]{:S(2)}, u32[]{:S(2)}) collective-permute-start(bf16[256,256]{1,0:T(8,128)(2,1)S(1)} %add_convert_fusion.1.refs_0_), channel_id=1, source_target_pairs={{0,16},{4,20},{8,24},{12,28},{16,0},{20,4},{24,8},{28,12},{1,17},{... | collective-permute-start | bytes 393224 | tf_op jit(solution)/shard_map/ppermute | solution.py:98
  72.0 1.5 %collective-permute-start.14 = (bf16[256,256]{1,0:T(8,128)(2,1)S(1)}, bf16[256,256]{1,0:T(8,128)(2,1)S(1)}, u32[]{:S(2)}, u32[]{:S(2)}) collective-permute-start(bf16[256,256]{1,0:T(8,128)(2,1)S(1)} %add_convert_fusion.1.refs_0_), channel_id=1, source_target_pairs={{0,24},{4,28},{8,16},{12,20},{16,8},{20,12},{24,0},{28,4},{1,25},{... | collective-permute-start | bytes 393224 | tf_op jit(solution)/shard_map/ppermute | solution.py:98
  73.4 1.9 %collective-permute-done.18 = bf16[256,256]{1,0:T(8,128)(2,1)S(1)} collective-permute-done((bf16[256,256]{1,0:T(8,128)(2,1)S(1)}, bf16[256,256]{1,0:T(8,128)(2,1)S(1)}, u32[]{:S(2)}, u32[]{:S(2)}) %collective-permute-start.18) | collective-permute-done | bytes 131104 | tf_op jit(solution)/shard_map/ppermute | solution.py:98
  75.5 3.6 %collective-permute-start.20 = (bf16[256,256]{1,0:T(8,128)(2,1)S(1)}, bf16[256,256]{1,0:T(8,128)(2,1)S(1)}, u32[]{:S(2)}, u32[]{:S(2)}) collective-permute-start(bf16[256,256]{1,0:T(8,128)(2,1)S(1)} %add_convert_fusion.refs_0_), channel_id=1, source_target_pairs={{0,16},{4,20},{8,24},{12,28},{16,0},{20,4},{24,8},{28,12},{1,17},{... | collective-permute-start | bytes 393224 | tf_op jit(solution)/shard_map/ppermute | solution.py:98
  79.2 2.2 %collective-permute-done.13.refs_2_ = bf16[256,256]{1,0:T(8,128)(2,1)S(1)} collective-permute-done((bf16[256,256]{1,0:T(8,128)(2,1)S(1)}, bf16[256,256]{1,0:T(8,128)(2,1)S(1)}, u32[]{:S(2)}, u32[]{:S(2)}) %collective-permute-start.13) | collective-permute-done | bytes 131104 | tf_op jit(solution)/shard_map/ppermute | solution.py:98
  81.4 13.1 %collective-permute-done.14.refs_3_ = bf16[256,256]{1,0:T(8,128)(2,1)S(1)} collective-permute-done((bf16[256,256]{1,0:T(8,128)(2,1)S(1)}, bf16[256,256]{1,0:T(8,128)(2,1)S(1)}, u32[]{:S(2)}, u32[]{:S(2)}) %collective-permute-start.14) | collective-permute-done | bytes 131104 | tf_op jit(solution)/shard_map/ppermute | solution.py:98
  97.3 2.6 %collective-permute-done.21.refs_3_ = bf16[256,256]{1,0:T(8,128)(2,1)S(1)} collective-permute-done((bf16[256,256]{1,0:T(8,128)(2,1)S(1)}, bf16[256,256]{1,0:T(8,128)(2,1)S(1)}, u32[]{:S(2)}, u32[]{:S(2)}) %collective-permute-start.21) | collective-permute-done | bytes 131104 | tf_op jit(solution)/shard_map/ppermute | solution.py:98
  102.3 5.6 %collective-permute-done.22 = bf16[384,256]{1,0:T(8,128)(2,1)S(1)} collective-permute-done((bf16[384,256]{1,0:T(8,128)(2,1)S(1)}, bf16[384,256]{1,0:T(8,128)(2,1)S(1)}, u32[]{:S(2)}, u32[]{:S(2)}) %collective-permute-start.22) | collective-permute-done | bytes 196640 | tf_op jit(solution)/shard_map/ppermute | solution.py:98
  (57 shorter events, 12.4 us)
Async XLA Ops:
  0.6 36.4 %copy-start.1 = (bf16[256,768]{1,0:T(8,128)(2,1)S(1)}, bf16[256,768]{1,0:T(8,128)(2,1)}, u32[]{:S(2)}) copy-start(bf16[256,768]{1,0:T(8,128)(2,1)} %q2_ref.3) | copy-start | bytes 1179652
  2.0 22.3 %collective-permute-start.6 = (bf16[1,768,256]{2,1,0:T(8,128)(2,1)S(1)}, bf16[1,768,256]{2,1,0:T(8,128)(2,1)S(1)}, u32[]{:S(2)}, u32[]{:S(2)}) collective-permute-start(bf16[1,768,256]{2,1,0:T(8,128)(2,1)S(1)} %bitcast.11), channel_id=1, source_target_pairs={{0,0},{1,8},{2,16},{3,24},{4,4},{5,12},{6,20},{7,28},{8,1},{9,9},{... | collective-permute-start | bytes 1179656 | tf_op jit(solution)/shard_map/ppermute | solution.py:98
  5.8 19.4 %collective-permute-start = (bf16[256,256]{1,0:T(8,128)(2,1)S(1)}, bf16[256,256]{1,0:T(8,128)(2,1)S(1)}, u32[]{:S(2)}, u32[]{:S(2)}) collective-permute-start(bf16[256,256]{1,0:T(8,128)(2,1)S(1)} %pad_maximum_fusion.4.b0_ref), channel_id=1, source_target_pairs={{0,12},{4,16},{8,20},{12,24},{16,28},{1,13},{5,17},{9,21},{13,25},... | collective-permute-start | bytes 393224 | tf_op jit(solution)/shard_map/ppermute | solution.py:98
  8.1 19.9 %collective-permute-start.1 = (bf16[256,256]{1,0:T(8,128)(2,1)S(1)}, bf16[256,256]{1,0:T(8,128)(2,1)S(1)}, u32[]{:S(2)}, u32[]{:S(2)}) collective-permute-start(bf16[256,256]{1,0:T(8,128)(2,1)S(1)} %pad_maximum_fusion.4.b0_ref), channel_id=1, source_target_pairs={{0,8},{4,12},{8,16},{12,20},{16,24},{20,28},{1,9},{5,13},{9,17},{1... | collective-permute-start | bytes 393224 | tf_op jit(solution)/shard_map/ppermute | solution.py:98
  12.8 24.3 %collective-permute-start.2 = (bf16[256,256]{1,0:T(8,128)(2,1)S(1)}, bf16[256,256]{1,0:T(8,128)(2,1)S(1)}, u32[]{:S(2)}, u32[]{:S(2)}) collective-permute-start(bf16[256,256]{1,0:T(8,128)(2,1)S(1)} %pad_maximum_fusion.4.b0_ref), channel_id=1, source_target_pairs={{0,4},{4,8},{8,12},{12,16},{16,20},{20,24},{24,28},{1,5},{5,9},{9,... | collective-permute-start | bytes 393224 | tf_op jit(solution)/shard_map/ppermute | solution.py:98
  14.8 33.9 %collective-permute-start.3 = (bf16[256,256]{1,0:T(8,128)(2,1)S(1)}, bf16[256,256]{1,0:T(8,128)(2,1)S(1)}, u32[]{:S(2)}, u32[]{:S(2)}) collective-permute-start(bf16[256,256]{1,0:T(8,128)(2,1)S(1)} %pad_maximum_fusion.5.b0_ref), channel_id=1, source_target_pairs={{0,12},{4,16},{8,20},{12,24},{16,28},{1,13},{5,17},{9,21},{13,25},... | collective-permute-start | bytes 393224 | tf_op jit(solution)/shard_map/ppermute | solution.py:98
  24.2 23.0 %collective-permute-start.7 = (bf16[1,768,256]{2,1,0:T(8,128)(2,1)S(1)}, bf16[1,768,256]{2,1,0:T(8,128)(2,1)S(1)}, u32[]{:S(2)}, u32[]{:S(2)}) collective-permute-start(bf16[1,768,256]{2,1,0:T(8,128)(2,1)S(1)} %collective-permute-done.6), channel_id=1, source_target_pairs={{0,2},{1,3},{2,0},{3,1},{4,6},{5,7},{6,4},{7,5},{8,10},{9,11},{10,... | collective-permute-start | bytes 1179656 | tf_op jit(solution)/shard_map/ppermute | solution.py:98
  25.2 25.5 %collective-permute-start.4 = (bf16[256,256]{1,0:T(8,128)(2,1)S(1)}, bf16[256,256]{1,0:T(8,128)(2,1)S(1)}, u32[]{:S(2)}, u32[]{:S(2)}) collective-permute-start(bf16[256,256]{1,0:T(8,128)(2,1)S(1)} %pad_maximum_fusion.5.b0_ref), channel_id=1, source_target_pairs={{0,8},{4,12},{8,16},{12,20},{16,24},{20,28},{1,9},{5,13},{9,17},{1... | collective-permute-start | bytes 393224 | tf_op jit(solution)/shard_map/ppermute | solution.py:98
  28.0 22.8 %collective-permute-start.5 = (bf16[256,256]{1,0:T(8,128)(2,1)S(1)}, bf16[256,256]{1,0:T(8,128)(2,1)S(1)}, u32[]{:S(2)}, u32[]{:S(2)}) collective-permute-start(bf16[256,256]{1,0:T(8,128)(2,1)S(1)} %pad_maximum_fusion.5.b0_ref), channel_id=1, source_target_pairs={{0,4},{4,8},{8,12},{12,16},{16,20},{20,24},{24,28},{1,5},{5,9},{9,... | collective-permute-start | bytes 393224 | tf_op jit(solution)/shard_map/ppermute | solution.py:98
  44.2 16.5 %collective-permute-start.10 = (bf16[256,256]{1,0:T(8,128)(2,1)S(1)}, bf16[256,256]{1,0:T(8,128)(2,1)S(1)}, u32[]{:S(2)}, u32[]{:S(2)}) collective-permute-start(bf16[256,256]{1,0:T(8,128)(2,1)S(1)} %get-tuple-element.25), channel_id=1, source_target_pairs={{8,0},{12,4},{16,8},{20,12},{24,16},{28,20},{9,1},{13,5},{17,9},{2... | collective-permute-start | bytes 393224 | tf_op jit(solution)/shard_map/ppermute | solution.py:98
  47.3 15.4 %collective-permute-start.11 = (bf16[256,256]{1,0:T(8,128)(2,1)S(1)}, bf16[256,256]{1,0:T(8,128)(2,1)S(1)}, u32[]{:S(2)}, u32[]{:S(2)}) collective-permute-start(bf16[256,256]{1,0:T(8,128)(2,1)S(1)} %get-tuple-element.26), channel_id=1, source_target_pairs={{12,0},{16,4},{20,8},{24,12},{28,16},{13,1},{17,5},{21,9},{25,13},... | collective-permute-start | bytes 393224 | tf_op jit(solution)/shard_map/ppermute | solution.py:98
  48.6 15.3 %collective-permute-start.9 = (bf16[256,256]{1,0:T(8,128)(2,1)S(1)}, bf16[256,256]{1,0:T(8,128)(2,1)S(1)}, u32[]{:S(2)}, u32[]{:S(2)}) collective-permute-start(bf16[256,256]{1,0:T(8,128)(2,1)S(1)} %get-tuple-element.24), channel_id=1, source_target_pairs={{4,0},{8,4},{12,8},{16,12},{20,16},{24,20},{28,24},{5,1},{9,5},{13... | collective-permute-start | bytes 393224 | tf_op jit(solution)/shard_map/ppermute | solution.py:98
  50.8 24.7 %collective-permute-start.8 = (bf16[2,768,256]{2,1,0:T(8,128)(2,1)S(1)}, bf16[2,768,256]{2,1,0:T(8,128)(2,1)S(1)}, u32[]{:S(2)}, u32[]{:S(2)}) collective-permute-start(bf16[2,768,256]{2,1,0:T(8,128)(2,1)S(1)} %pad_maximum_fusion), channel_id=1, source_target_pairs={{0,1},{1,0},{2,3},{3,2},{4,5},{5,4},{6,7},{7,6},{8,9},{9,8},{10,11... | collective-permute-start | bytes 2359304 | tf_op jit(solution)/shard_map/ppermute | solution.py:98
  57.9 9.6 %collective-permute-start.16 = (bf16[256,256]{1,0:T(8,128)(2,1)S(1)}, bf16[256,256]{1,0:T(8,128)(2,1)S(1)}, u32[]{:S(2)}, u32[]{:S(2)}) collective-permute-start(bf16[256,256]{1,0:T(8,128)(2,1)S(1)} %get-tuple-element.30), channel_id=1, source_target_pairs={{4,0},{8,4},{12,8},{16,12},{20,16},{24,20},{28,24},{5,1},{9,5},{13... | collective-permute-start | bytes 393224 | tf_op jit(solution)/shard_map/ppermute | solution.py:98
  60.7 11.3 %collective-permute-start.17 = (bf16[256,256]{1,0:T(8,128)(2,1)S(1)}, bf16[256,256]{1,0:T(8,128)(2,1)S(1)}, u32[]{:S(2)}, u32[]{:S(2)}) collective-permute-start(bf16[256,256]{1,0:T(8,128)(2,1)S(1)} %get-tuple-element.31), channel_id=1, source_target_pairs={{8,0},{12,4},{16,8},{20,12},{24,16},{28,20},{9,1},{13,5},{17,9},{2... | collective-permute-start | bytes 393224 | tf_op jit(solution)/shard_map/ppermute | solution.py:98
  62.6 12.7 %collective-permute-start.18 = (bf16[256,256]{1,0:T(8,128)(2,1)S(1)}, bf16[256,256]{1,0:T(8,128)(2,1)S(1)}, u32[]{:S(2)}, u32[]{:S(2)}) collective-permute-start(bf16[256,256]{1,0:T(8,128)(2,1)S(1)} %get-tuple-element.32), channel_id=1, source_target_pairs={{12,0},{16,4},{20,8},{24,12},{28,16},{13,1},{17,5},{21,9},{25,13},... | collective-permute-start | bytes 393224 | tf_op jit(solution)/shard_map/ppermute | solution.py:98
  64.0 15.1 %collective-permute-start.12 = (bf16[256,256]{1,0:T(8,128)(2,1)S(1)}, bf16[256,256]{1,0:T(8,128)(2,1)S(1)}, u32[]{:S(2)}, u32[]{:S(2)}) collective-permute-start(bf16[256,256]{1,0:T(8,128)(2,1)S(1)} %add_convert_fusion.1.refs_0_), channel_id=1, source_target_pairs={{0,8},{4,12},{8,0},{12,4},{16,24},{20,28},{24,16},{28,20},{1,9},{5... | collective-permute-start | bytes 393224 | tf_op jit(solution)/shard_map/ppermute | solution.py:98
  67.5 13.9 %collective-permute-start.13 = (bf16[256,256]{1,0:T(8,128)(2,1)S(1)}, bf16[256,256]{1,0:T(8,128)(2,1)S(1)}, u32[]{:S(2)}, u32[]{:S(2)}) collective-permute-start(bf16[256,256]{1,0:T(8,128)(2,1)S(1)} %add_convert_fusion.1.refs_0_), channel_id=1, source_target_pairs={{0,16},{4,20},{8,24},{12,28},{16,0},{20,4},{24,8},{28,12},{1,17},{... | collective-permute-start | bytes 393224 | tf_op jit(solution)/shard_map/ppermute | solution.py:98
  72.0 22.5 %collective-permute-start.14 = (bf16[256,256]{1,0:T(8,128)(2,1)S(1)}, bf16[256,256]{1,0:T(8,128)(2,1)S(1)}, u32[]{:S(2)}, u32[]{:S(2)}) collective-permute-start(bf16[256,256]{1,0:T(8,128)(2,1)S(1)} %add_convert_fusion.1.refs_0_), channel_id=1, source_target_pairs={{0,24},{4,28},{8,16},{12,20},{16,8},{20,12},{24,0},{28,4},{1,25},{... | collective-permute-start | bytes 393224 | tf_op jit(solution)/shard_map/ppermute | solution.py:98
  75.4 21.9 %collective-permute-start.19 = (bf16[256,256]{1,0:T(8,128)(2,1)S(1)}, bf16[256,256]{1,0:T(8,128)(2,1)S(1)}, u32[]{:S(2)}, u32[]{:S(2)}) collective-permute-start(bf16[256,256]{1,0:T(8,128)(2,1)S(1)} %add_convert_fusion.refs_0_), channel_id=1, source_target_pairs={{0,8},{4,12},{8,0},{12,4},{16,24},{20,28},{24,16},{28,20},{1,9},{5... | collective-permute-start | bytes 393224 | tf_op jit(solution)/shard_map/ppermute | solution.py:98
  75.5 21.8 %collective-permute-start.20 = (bf16[256,256]{1,0:T(8,128)(2,1)S(1)}, bf16[256,256]{1,0:T(8,128)(2,1)S(1)}, u32[]{:S(2)}, u32[]{:S(2)}) collective-permute-start(bf16[256,256]{1,0:T(8,128)(2,1)S(1)} %add_convert_fusion.refs_0_), channel_id=1, source_target_pairs={{0,16},{4,20},{8,24},{12,28},{16,0},{20,4},{24,8},{28,12},{1,17},{... | collective-permute-start | bytes 393224 | tf_op jit(solution)/shard_map/ppermute | solution.py:98
  79.1 20.8 %collective-permute-start.21 = (bf16[256,256]{1,0:T(8,128)(2,1)S(1)}, bf16[256,256]{1,0:T(8,128)(2,1)S(1)}, u32[]{:S(2)}, u32[]{:S(2)}) collective-permute-start(bf16[256,256]{1,0:T(8,128)(2,1)S(1)} %add_convert_fusion.refs_0_), channel_id=1, source_target_pairs={{0,24},{4,28},{8,16},{12,20},{16,8},{20,12},{24,0},{28,4},{1,25},{... | collective-permute-start | bytes 393224 | tf_op jit(solution)/shard_map/ppermute | solution.py:98
  95.6 6.6 %collective-permute-start.15 = (bf16[384,256]{1,0:T(8,128)(2,1)S(1)}, bf16[384,256]{1,0:T(8,128)(2,1)S(1)}, u32[]{:S(2)}, u32[]{:S(2)}) collective-permute-start(bf16[384,256]{1,0:T(8,128)(2,1)S(1)} %bitcast.9), channel_id=1, source_target_pairs={{0,4},{4,0},{8,12},{12,8},{16,20},{20,16},{24,28},{28,24},{1,5},{5... | collective-permute-start | bytes 589832 | tf_op jit(solution)/shard_map/ppermute | solution.py:98
  101.1 6.8 %collective-permute-start.22 = (bf16[384,256]{1,0:T(8,128)(2,1)S(1)}, bf16[384,256]{1,0:T(8,128)(2,1)S(1)}, u32[]{:S(2)}, u32[]{:S(2)}) collective-permute-start(bf16[384,256]{1,0:T(8,128)(2,1)S(1)} %bitcast.10), channel_id=1, source_target_pairs={{0,4},{4,0},{8,12},{12,8},{16,20},{20,16},{24,28},{28,24},{1,5},{5... | collective-permute-start | bytes 589832 | tf_op jit(solution)/shard_map/ppermute | solution.py:98
  (5 other events, 169.3 us)

commit v2 on v1

v2 whole, which is shorter than its diff:
```python
import functools
import math

import jax
import jax.numpy as jnp
from jax import lax
from jax.experimental import pallas as pl
from jax.experimental.pallas import tpu as pltpu
from jax.sharding import PartitionSpec as P

HD = 128
REACH = 3
NT = (((1,), (1,)), ((), ()))


def attend(rows, group, shard, lens_ref, kv_ref, kt_ref, bias_ref, acc_ref, held_ref, made_ref, ready):
    window = (REACH + 1) * rows
    half = rows // 2
    span = window - half
    scale = 1.0 / math.sqrt(HD)
    kt_ref[...] = kv_ref[:, :HD].T
    base = shard * rows
    places = base + lax.broadcasted_iota(jnp.int32, (1, rows), 1)

    def later(i, carry):
        end, first = carry
        end = end + lens_ref[i]
        return end, jnp.where(places >= end, end, first)

    _, first = lax.fori_loop(0, lens_ref.shape[0], later, (jnp.int32(0), jnp.zeros((1, rows), jnp.int32)))
    for side in range(2):
        keys = base - REACH * rows + side * half + lax.broadcasted_iota(jnp.int32, (span, half), 0)
        own = slice(side * half, (side + 1) * half)
        allowed = (keys >= first[:, own]) & (keys <= places[:, own])
        bias_ref[side] = jnp.where(allowed, 0.0, -1e30)
    ready()
    units = [(l, j) for l in range(2) for j in range(group)]
    chunks = [units[n:n + 2] for n in range(0, len(units), 2)]
    steps = [(side, n) for side in range(2) for n in range(len(chunks))]

    def operands(side, n):
        r = slice(side * half, (side + 1) * half)
        q = jnp.concatenate([held_ref[l, r, j * HD:(j + 1) * HD] for l, j in chunks[n]], axis=0)
        g = jnp.concatenate([held_ref[2 + l, r, j * HD:(j + 1) * HD] for l, j in chunks[n]], axis=0)
        return q, g

    def products(side, n):
        w = slice(side * half, side * half + span)
        q, g = operands(side, n)
        s = lax.dot_general(kv_ref[w, :HD], q, NT, preferred_element_type=jnp.float32)
        dp = lax.dot_general(kv_ref[w, HD:], g, NT, preferred_element_type=jnp.float32)
        return s, dp

    ahead = products(*steps[0])
    for at, (side, n) in enumerate(steps):
        s, dp = ahead
        if at + 1 < len(steps):
            ahead = products(*steps[at + 1])
        w = slice(side * half, side * half + span)
        r = slice(side * half, (side + 1) * half)
        bias = bias_ref[side]
        s = s * (scale * math.log2(math.e)) + jnp.concatenate([bias] * len(chunks[n]), axis=1)
        raised = jnp.exp2(s - jnp.max(s, axis=0, keepdims=True))
        p = raised * (1.0 / jnp.sum(raised, axis=0, keepdims=True))
        ph = p.astype(jnp.bfloat16)
        delta = jnp.sum(ph.astype(jnp.float32) * dp, axis=0, keepdims=True)
        ds = (p * (dp - delta)).astype(jnp.bfloat16)
        q, g = operands(side, n)
        if side == 0 and n == 0:
            acc_ref[span:, :] = jnp.zeros((half, 2 * HD), jnp.float32)
            acc_ref[w, HD:] = jnp.dot(ph, g, preferred_element_type=jnp.float32)
            acc_ref[w, :HD] = jnp.dot(ds, q, preferred_element_type=jnp.float32)
        else:
            acc_ref[w, HD:] += jnp.dot(ph, g, preferred_element_type=jnp.float32)
            acc_ref[w, :HD] += jnp.dot(ds, q, preferred_element_type=jnp.float32)
        dq = (jnp.dot(kt_ref[:, w], ds, preferred_element_type=jnp.float32) * scale).T.astype(jnp.bfloat16)
        for i, (l, j) in enumerate(chunks[n]):
            made_ref[l, r, j * HD:(j + 1) * HD] = dq[i * half:(i + 1) * half]


def attend_scratch(rows):
    keys = (REACH + 1) * rows
    return [pltpu.VMEM((keys, 2 * HD), jnp.bfloat16), pltpu.VMEM((HD, keys), jnp.bfloat16),
            pltpu.VMEM((2, keys - rows // 2, rows // 2), jnp.float32)]


def chosen(lane, kv_ref, i, ref, other):
    rows = ref.shape[0]
    if ref is other:
        kv_ref[i * rows:(i + 1) * rows, :] = ref[...]
        return

    @pl.when(lane == 0)
    def _():
        kv_ref[i * rows:(i + 1) * rows, :] = ref[...]

    @pl.when(lane == 1)
    def _():
        kv_ref[i * rows:(i + 1) * rows, :] = other[...]


def fetched(arrays, columns, held_ref, sems):
    copies = [pltpu.make_async_copy(ref.at[:, columns], held_ref.at[i], sems.at[i]) for i, ref in enumerate(arrays)]
    for copy in copies:
        copy.start()

    def ready():
        for copy in copies:
            copy.wait()

    return ready


def scaled(term):
    return jnp.concatenate([term[:, :HD] * (1.0 / math.sqrt(HD)), term[:, HD:]], axis=1)


def whole_kernel(head, rows, group, here_ref, lens_ref, q1, q2, g1, g2, b3, b2, b1, b0,
                 made_ref, f3_ref, f2_ref, f1_ref, own_ref, kv_ref, kt_ref, bias_ref, acc_ref, held_ref, sems):
    ready = fetched((q1, q2, g1, g2), slice(head * group * HD, (head + 1) * group * HD), held_ref, sems)
    for i, ref in enumerate((b3, b2, b1, b0)):
        kv_ref[i * rows:(i + 1) * rows, :] = ref[...]
    attend(rows, group, here_ref[0], lens_ref, kv_ref, kt_ref, bias_ref, acc_ref, held_ref, made_ref, ready)
    for i, ref in enumerate((f3_ref, f2_ref, f1_ref, own_ref)):
        ref[...] = scaled(acc_ref[i * rows:(i + 1) * rows, :]).astype(ref.dtype)


def first_kernel(rows, group, here_ref, lens_ref, q1, q2, g1, g2, far, lifted, mine, got,
                 made_ref, acc_ref, kv_ref, kt_ref, bias_ref, held_ref, sems):
    lane = here_ref[0] % 2
    ready = fetched((q1, q2, g1, g2), pl.ds(pl.multiple_of(lane * group * HD, HD), group * HD), held_ref, sems)
    along, crosswise = lifted.at[0], lifted.at[1]
    for i, pair in enumerate(((far, crosswise), (along, along), (crosswise, got), (mine, mine))):
        chosen(lane, kv_ref, i, *pair)
    attend(rows, group, here_ref[0], lens_ref, kv_ref, kt_ref, bias_ref, acc_ref, held_ref, made_ref, ready)


def second_kernel(rows, group, here_ref, lens_ref, held_ref, far, lifted, mine, got, before_ref,
                  made_ref, far_ref, pair_ref, own_ref, kv_ref, kt_ref, bias_ref, acc_ref):
    lane = here_ref[0] % 2
    along, crosswise = lifted.at[0], lifted.at[1]
    for i, pair in enumerate(((along, far), (crosswise, crosswise), (mine, along), (got, got))):
        chosen(lane, kv_ref, i, *pair)
    attend(rows, group, here_ref[0] + 1 - 2 * lane, lens_ref, kv_ref, kt_ref, bias_ref, acc_ref, held_ref, made_ref, lambda: None)

    def merged(even_ref, odd_ref):
        block = lambda ref, i: ref[i * rows:(i + 1) * rows, :]
        far_ref[...] = scaled(block(even_ref, 0)).astype(far_ref.dtype)
        for i in range(2):
            pair_ref[i] = scaled(block(even_ref, 1 + i) + block(odd_ref, i)).astype(pair_ref.dtype)
        own_ref[0] = scaled(block(even_ref, 3) + block(odd_ref, 2))
        own_ref[1] = scaled(block(odd_ref, 3))

    @pl.when(lane == 0)
    def _():
        merged(before_ref, acc_ref)

    @pl.when(lane == 1)
    def _():
        merged(acc_ref, before_ref)


def called(kernel, name, operands, kinds, outs, scratch):
    places = {"s": pltpu.SMEM, "v": pltpu.VMEM, "h": pltpu.HBM}
    return pl.pallas_call(
        kernel,
        in_specs=[pl.BlockSpec(memory_space=places[k]) for k in kinds],
        out_specs=[pl.BlockSpec(memory_space=pltpu.VMEM)] * len(outs),
        out_shape=[jax.ShapeDtypeStruct(shape, dtype) for shape, dtype in outs],
        scratch_shapes=scratch,
        compiler_params=pltpu.CompilerParams(vmem_limit_bytes=44 * 1024 * 1024),
        cost_estimate=pl.CostEstimate(flops=1 << 15, bytes_accessed=1 << 15, transcendentals=0),
        name=name,
    )(*operands)


def moved(value, axis, place):
    pairs = [(i, place(i)) for i in range(lax.axis_size(axis))]
    return lax.ppermute(value, axis, [(i, j) for i, j in pairs if j is not None])


def after(value, *earlier):
    return lax.optimization_barrier((value,) + earlier)[0]


def gathered(kv_grads, heads, lanes):
    return [kv_grads] + [
        moved(kv_grads, "tok", lambda t, j=j: ((t // lanes) ^ j) * lanes + t % lanes) for j in range(1, heads)]


def project_kernel(count, paired, picks_ref, *refs):
    blocks, hids, (own_ref, away_ref) = refs[:count], refs[count:-2], refs[-2:]
    line, head, mine = picks_ref[0], picks_ref[1], picks_ref[2]
    total = None
    for j, block in enumerate(blocks):
        if paired:
            near = (line ^ j) % 2 == head % 2
            y = head // 2
            terms = []
            for e in range(2):
                slots = [4 * e + 2 * (y ^ q) + j // 2 for q in range(2)]
                pieces = [jnp.where(near, hids[0][slot], hids[1][slot]) for slot in slots]
                terms.append((jnp.concatenate(pieces, axis=1), block[mine ^ e]))
        else:
            slot, step = 0, 1
            while step < count:
                slot = 2 * slot + ((line ^ j ^ head) // step) % 2
                step *= 2
            terms = [(hids[0][slot], block[...])]
        for turned, grads in terms:
            term = jnp.dot(turned, grads, preferred_element_type=jnp.float32)
            total = term if total is None else total + term
    lanes, part = away_ref.shape[0] + 1, own_ref.shape[0]
    own_ref[...] = jnp.zeros_like(own_ref)
    for d in range(lanes):
        piece = total[d * part:(d + 1) * part]

        @pl.when(mine == d)
        def _():
            own_ref[...] = piece

        for e in range(1, lanes):
            @pl.when((mine ^ e) == d)
            def _():
                away_ref[e - 1] = piece.astype(jnp.bfloat16)


def project(picks, hids, blocks, lanes):
    part = hids[0].shape[-2] // lanes
    columns = blocks[0].shape[-1]
    return called(
        functools.partial(project_kernel, len(blocks), len(hids) > 1), "project", [picks, *blocks, *hids],
        "s" + "v" * (len(blocks) + len(hids)),
        [((part, columns), jnp.float32), ((lanes - 1, part, columns), jnp.bfloat16)], [])


def general(place, line, lane, head, heads, tokens, lanes, kv_heads, lens, arrays, stacked, hidden_states):
    def crossed(i):
        t, h = i // heads, i % heads
        return (h * lanes + t % lanes) * heads + t // lanes

    hid = moved(hidden_states.T[None], ("tok", "head"), crossed)
    step = heads // 2
    while step:
        hid = jnp.concatenate([hid, moved(hid, "head", lambda h: h ^ step)], axis=0)
        step //= 2
    picks = jnp.stack([line, head, lane]).astype(jnp.int32)
    rows, width = arrays[0].shape
    group = width // (kv_heads * HD)
    block = (rows, 2 * HD)
    firsts, seconds, parts = [], [], []
    for c, own in enumerate(stacked):
        window = [moved(own, "tok", lambda t, s=s: t + s if t + s < tokens else None) for s in range(REACH, 0, -1)] + [own]
        made, *far, total = called(
            functools.partial(whole_kernel, c, rows, group), "attend", [place, lens, *arrays, *window],
            "ss" + "h" * 4 + "v" * 4,
            [((2, rows, group * HD), jnp.bfloat16)] + [(block, jnp.bfloat16)] * REACH + [(block, jnp.float32)],
            attend_scratch(rows) + [pltpu.VMEM(((REACH + 1) * rows, 2 * HD), jnp.float32),
                                    pltpu.VMEM((4, rows, group * HD), jnp.bfloat16), pltpu.SemaphoreType.DMA((4,))])
        firsts.append(made[0])
        seconds.append(made[1])
        for s in range(1, REACH + 1):
            back = moved(far[REACH - s], "tok", lambda t, s=s: t - s if t >= s else None)
            total = total + back.astype(jnp.float32)
        mine, away = project(picks, [hid], gathered(total.astype(jnp.bfloat16), heads, lanes), lanes)
        for d in range(1, lanes):
            mine = mine + moved(away[d - 1], "tok", lambda t, d=d: t ^ d).astype(jnp.float32)
        parts.append(mine)
    return tuple(jnp.concatenate(x, axis=1) for x in (firsts, seconds, parts))


def paired(place, line, lane, head, heads, tokens, lanes, kv_heads, lens, arrays, stacked, hidden_states):
    both = ("tok", "head")
    rows, width = arrays[0].shape
    group = width // (kv_heads * HD)
    wide = group * HD
    even = lane == 0

    def mine_and_other(a, b):
        return jnp.where(even, a, b), jnp.where(even, b, a)

    def up(value, lines):
        return moved(value, "tok", lambda t: t + lines * lanes if t + lines * lanes < tokens else None)

    def down(value, lines):
        return moved(value, "tok", lambda t: t - lines * lanes if t >= lines * lanes else None)

    def over(value):
        return moved(value, "tok", lambda t: t ^ 1)

    def crossed(flip):
        def place_of(i):
            t, h = i // heads, i % heads
            z, c = t // lanes, h % 2
            return (((z // 2) ^ flip) * 2 + c) * lanes * heads + (t % lanes) * heads + (h // 2) * 2 + z % 2
        return place_of

    given = jnp.where(even, stacked[1], stacked[0])
    mine = jnp.where(even, after(stacked[0], given), stacked[1])
    got = over(given)
    risen = jnp.stack([mine, got])
    lifted = up(risen, 1)
    far = up(jnp.where(even, got, mine), 2)
    asked = over(jnp.stack([jnp.where(even, a[:, wide:], a[:, :wide]) for a in (after(x, given) for x in arrays)]))
    y = head // 2
    half = rows // 2
    kept, lent = (lax.dynamic_slice_in_dim(hidden_states, at * half, half, 0) for at in (y, 1 - y))
    lent = moved(lent, "head", lambda h: h ^ 2)
    own_line = (line // 2) == y
    afar = moved(after(jnp.where(own_line, lent, kept), lifted, far), both, crossed(1))

    window = [far, lifted, mine, got]
    keys = (REACH + 1) * rows
    made, sums = called(
        functools.partial(first_kernel, rows, group), "attend_own", [place, lens, *arrays, *window], "ss" + "h" * 4 + "v" * 4,
        [((2, rows, wide), jnp.bfloat16), ((keys, 2 * HD), jnp.float32)],
        attend_scratch(rows) + [pltpu.VMEM((4, rows, wide), jnp.bfloat16), pltpu.SemaphoreType.DMA((4,))])
    nearby = moved(after(jnp.where(own_line, kept, lent), sums), both, crossed(0))
    made_other, farther, nearer, own = called(
        functools.partial(second_kernel, rows, group), "attend_other", [place, lens, asked, *window, after(sums, afar)],
        "ss" + "v" * 6,
        [((2, rows, wide), jnp.bfloat16), ((rows, 2 * HD), jnp.bfloat16), ((2, rows, 2 * HD), jnp.bfloat16),
         ((2, rows, 2 * HD), jnp.float32)],
        attend_scratch(rows) + [pltpu.VMEM((keys, 2 * HD), jnp.float32)])

    one, two = down(nearer, 1), down(farther, 2)
    hops = jnp.swapaxes(jnp.stack([nearby, after(afar, own)]), 1, 2)
    beside = over(hops)
    hids = [hops, moved(hops, "head", lambda h: h ^ 2), beside, moved(beside, "head", lambda h: h ^ 2)]
    total = (own + one.astype(jnp.float32)).at[1].add(two.astype(jnp.float32)).astype(jnp.bfloat16)
    across = moved(total, "tok", lambda t: t ^ (2 * lanes))
    blocks = [total, moved(total, "tok", lambda t: t ^ lanes), across, moved(across, "tok", lambda t: t ^ lanes)]
    sent = over(after(made_other, total))
    hids = jnp.concatenate([after(hids[0], *blocks[1:3])] + hids[1:], axis=0)
    firsts, seconds = (jnp.concatenate(mine_and_other(after(made[l], hids), sent[l]), axis=1) for l in range(2))

    picks = jnp.stack([line, head, lane]).astype(jnp.int32)
    kept, away = project(picks, [hids, moved(hids, "head", lambda h: h ^ 1)], blocks, lanes)
    came = over(away[0]).astype(jnp.float32)
    return (firsts, seconds, jnp.concatenate(mine_and_other(kept, came), axis=1))


def body(queries_first, queries_second, grads_first, grads_second, key_states, value_states, doc_lengths, hidden_states):
    kv_heads = key_states.shape[1] // HD
    tokens, heads = lax.axis_size("tok"), lax.axis_size("head")
    lanes = tokens // heads
    here, head = lax.axis_index("tok"), lax.axis_index("head")
    arrays = (queries_first, queries_second, grads_first, grads_second)
    stacked = [jnp.concatenate([key_states[:, c * HD:(c + 1) * HD], value_states[:, c * HD:(c + 1) * HD]], axis=1)
               for c in range(kv_heads)]
    plan = paired if (lanes, heads, kv_heads, REACH) == (2, 4, 2, 3) else general
    return plan(here.reshape(1).astype(jnp.int32), here // lanes, here % lanes, head, heads, tokens, lanes, kv_heads,
                doc_lengths, arrays, stacked, hidden_states)


def solution(mesh):
    split = P("tok", "head")
    return jax.shard_map(
        body,
        mesh=mesh,
        in_specs=(split,) * 6 + (P(), split),
        out_specs=(split,) * 3,
        check_vma=False,
    )
```

time: 109 us -> 94.2 us (0.86)
  the two profiles are of different devices: /device:TPU:12 before, /device:TPU:0 now
where the time goes in v2:
time: 94.2 us; the launch traced here: 93.9 us
  waiting for transfers between devices  44.4 us (47%)
  starting transfers between devices  25.2 us (27%)
  Pallas kernels  13.3 us (14%)
  other arithmetic  5.8 us (6%)
  local copies, waits for them, and re-layouts  4.19 us (4%)
  between operations  1.03 us (1%)
    ppermute x18, waiting for transfers between devices, moved(): lax.ppermute(value, axis, [(i, j) for i, j in pairs if j is not None])  44.4 us
    ppermute x18, starting transfers between devices, moved(): lax.ppermute(value, axis, [(i, j) for i, j in pairs if j is not None])  25.2 us
    pallas_call x3, Pallas kernels, called(): pl.pallas_call(kernel, in_specs=[pl.BlockSpec(memory_space=places[k]) for...  13.3 us
  transfers between devices with their start and end apart: 18, of which 8 were waited for; matrix products, arithmetic and copies ran while one was open for 7% of the time, Pallas kernels for 13%

profile of v2, /device:TPU:0, one launch (start us, length us, event | category | flops | bytes accessed | tf_op | source)
XLA Modules:
  0.0 93.9 jit_solution(10308435168990635999)
XLA Ops:
  2.7 3.0 %collective-permute-start = (bf16[256,256]{1,0:T(8,128)(2,1)S(1)}, bf16[256,256]{1,0:T(8,128)(2,1)S(1)}, u32[]{:S(2)}, u32[]{:S(2)}) collective-permute-start(bf16[256,256]{1,0:T(8,128)(2,1)S(1)} %get-tuple-element.74), channel_id=1, source_target_pairs={{0,4},{4,0},{8,12},{12,8},{16,20},{20,16},{24,28},{28,24},{1,5},{5... | collective-permute-start | bytes 393224 | tf_op jit(solution)/shard_map/ppermute | solution.py:179
  5.7 1.0 %constant_dynamic-slice_fusion.1 = (bf16[128,768]{1,0:T(8,128)(2,1)S(1)}, bf16[128,768]{1,0:T(8,128)(2,1)S(1)}) fusion(bf16[256,768]{1,0:T(8,128)(2,1)} %param.17, s32[]{:T(128)S(6)} %select_n.109, s32[]{:T(128)S(6)} %select_n.110), kind=kLoop, calls=%fused_computation.35 | loop fusion | bytes 786440 | tf_op jit(solution)/shard_map/dynamic_slice | solution.py:307
  7.5 1.5 %collective-permute-start.3 = (bf16[128,768]{0,1:T(8,128)(2,1)}, bf16[128,768]{0,1:T(8,128)(2,1)}, u32[]{:S(2)}, u32[]{:S(2)}) collective-permute-start(bf16[128,768]{0,1:T(8,128)(2,1)} %copy.14), channel_id=1, source_target_pairs={{0,2},{1,3},{2,0},{3,1},{4,6},{5,7},{6,4},{7,5},{8,10},{9,11},{10,... | collective-permute-start | bytes 589832 | tf_op jit(solution)/shard_map/ppermute | solution.py:179
  9.2 1.0 %pad_maximum_fusion = bf16[4,256,384]{2,1,0:T(8,128)(2,1)} fusion(bf16[1,256,384]{2,1,0:T(8,128)(2,1)S(1)} %get-tuple-element.79, bf16[1,256,384]{2,1,0:T(8,128)(2,1)S(1)} %get-tuple-element.80, bf16[1,256,384]{2,1,0:T(8,128)(2,1)S(1)} %get-tuple-element.81, bf16[1,256,384]{2,1,0:T(8,128)(2,1)S(1)} %get-tuple-element.82), kind=kLoop, calls=%fused_computation | loop fusion | flops 1179648 | bytes 1572864 | tf_op jit(solution)/shard_map/stack | solution.py:304
  11.5 3.5 %collective-permute-start.2 = (bf16[2,256,256]{2,1,0:T(8,128)(2,1)S(1)}, bf16[2,256,256]{2,1,0:T(8,128)(2,1)S(1)}, u32[]{:S(2)}, u32[]{:S(2)}) collective-permute-start(bf16[2,256,256]{2,1,0:T(8,128)(2,1)S(1)} %pad_maximum_fusion.4), channel_id=1, source_target_pairs={{0,8},{4,12},{8,16},{12,20},{16,24},{20,28},{1,9},{5,13},{9,17},{1... | collective-permute-start | bytes 786440 | tf_op jit(solution)/shard_map/ppermute | solution.py:179
  15.2 4.5 %collective-permute-start.1 = (bf16[256,256]{1,0:T(8,128)(2,1)}, bf16[256,256]{1,0:T(8,128)(2,1)S(1)}, u32[]{:S(2)}, u32[]{:S(2)}) collective-permute-start(bf16[256,256]{1,0:T(8,128)(2,1)} %get-tuple-element.57), channel_id=1, source_target_pairs={{0,16},{4,20},{8,24},{12,28},{1,17},{5,21},{9,25},{13,29},{2,18},{... | collective-permute-start | bytes 393224 | tf_op jit(solution)/shard_map/ppermute | solution.py:179
  19.7 1.0 %broadcast_select_fusion.1 = (bf16[128,768]{0,1:T(8,128)(2,1)S(1)}, bf16[128,768]{0,1:T(8,128)(2,1)S(1)}) fusion(bf16[128,768]{0,1:T(8,128)(2,1)S(1)} %copy.13, bf16[128,768]{0,1:T(8,128)(2,1)} %collective-permute-done.3, pred[]{:T(512)S(6)} %eq.9), kind=kLoop, calls=%fused_computation.20 | loop fusion | flops 196608 | bytes 786433 | tf_op jit(solution)/shard_map/jit(_where)/select_n | solution.py:318
  20.7 2.0 %collective-permute-done.1.far = bf16[256,256]{1,0:T(8,128)(2,1)S(1)} collective-permute-done((bf16[256,256]{1,0:T(8,128)(2,1)}, bf16[256,256]{1,0:T(8,128)(2,1)S(1)}, u32[]{:S(2)}, u32[]{:S(2)}) %collective-permute-start.1) | collective-permute-done | bytes 131104 | tf_op jit(solution)/shard_map/ppermute | solution.py:179
  22.7 4.7 %collective-permute-start.5 = (bf16[128,768]{0,1:T(8,128)(2,1)S(1)}, bf16[128,768]{0,1:T(8,128)(2,1)S(1)}, u32[]{:S(2)}, u32[]{:S(2)}) collective-permute-start(bf16[128,768]{0,1:T(8,128)(2,1)S(1)} %get-tuple-element.40), channel_id=1, source_target_pairs={{0,16},{1,24},{2,18},{3,26},{4,20},{5,28},{6,22},{7,30},{8,17},{9,... | collective-permute-start | bytes 589832 | tf_op jit(solution)/shard_map/ppermute | solution.py:179
  27.4 6.0 %attend_own.1 = (bf16[2,256,384]{2,1,0:T(8,128)(2,1)S(1)}, f32[1024,256]{1,0:T(8,128)S(1)}) custom-call(s32[1]{0:T(128)} %bitcast.here_ref, s32[8]{0:T(128)S(1)} %copy-done.4, bf16[256,768]{1,0:T(8,128)(2,1)S(1)} %copy-done, bf16[256,768]{1,0:T(8,128)(2,1)S(1)} %copy-done.1, bf16[256,768]{1,0:T(8,128)(2,1)S(1)} %copy-done.2, bf16[256,768]{1,0:T(8,128)(2,1)S(1)} %copy-done.3, ...), custom_call_target="tpu_custom_call" | custom-call | flops 32768 | bytes 32768 | tf_op jit(solution)/shard_map/attend_own/pallas_call | solution.py:165
  34.1 2.6 %collective-permute-done.5 = bf16[128,768]{0,1:T(8,128)(2,1)S(1)} collective-permute-done((bf16[128,768]{0,1:T(8,128)(2,1)S(1)}, bf16[128,768]{0,1:T(8,128)(2,1)S(1)}, u32[]{:S(2)}, u32[]{:S(2)}) %collective-permute-start.5) | collective-permute-done | bytes 196640 | tf_op jit(solution)/shard_map/ppermute | solution.py:179
  36.7 5.8 %attend_other.1 = (bf16[2,256,384]{2,1,0:T(8,128)(2,1)S(1)}, bf16[256,256]{1,0:T(8,128)(2,1)S(1)}, bf16[2,256,256]{2,1,0:T(8,128)(2,1)S(1)}, f32[2,256,256]{2,1,0:T(8,128)S(1)}) custom-call(s32[1]{0:T(128)} %bitcast.here_ref, s32[8]{0:T(128)S(1)} %copy-done.4, bf16[4,256,384]{2,1,0:T(8,128)(2,1)S(1)} %collective-permute-done.6.held_ref, ...), custom_call_target="tpu_custom_call" | custom-call | flops 32768 | bytes 32768 | tf_op jit(solution)/shard_map/attend_other/pallas_call | solution.py:165
  42.5 1.5 %collective-permute-start.7 = (bf16[2,256,256]{2,1,0:T(8,128)(2,1)S(1)}, bf16[2,256,256]{2,1,0:T(8,128)(2,1)S(1)}, u32[]{:S(2)}, u32[]{:S(2)}) collective-permute-start(bf16[2,256,256]{2,1,0:T(8,128)(2,1)S(1)} %get-tuple-element.48), channel_id=1, source_target_pairs={{8,0},{12,4},{16,8},{20,12},{24,16},{28,20},{9,1},{13,5},{17,9},{2... | collective-permute-start | bytes 786440 | tf_op jit(solution)/shard_map/ppermute | solution.py:179
  44.6 1.5 %collective-permute-start.12 = (bf16[2,768,128]{2,1,0:T(8,128)(2,1)S(1)}, bf16[2,768,128]{2,1,0:T(8,128)(2,1)S(1)}, u32[]{:S(2)}, u32[]{:S(2)}) collective-permute-start(bf16[2,768,128]{2,1,0:T(8,128)(2,1)S(1)} %maximum_bitcast_fusion), channel_id=1, source_target_pairs={{0,4},{4,0},{8,12},{12,8},{16,20},{20,16},{24,28},{28,24},{1,5},{5... | collective-permute-start | bytes 1179656 | tf_op jit(solution)/shard_map/ppermute | solution.py:179
  46.1 1.3 %collective-permute-start.8 = (bf16[256,256]{1,0:T(8,128)(2,1)S(1)}, bf16[256,256]{1,0:T(8,128)(2,1)S(1)}, u32[]{:S(2)}, u32[]{:S(2)}) collective-permute-start(bf16[256,256]{1,0:T(8,128)(2,1)S(1)} %get-tuple-element.49), channel_id=1, source_target_pairs={{16,0},{20,4},{24,8},{28,12},{17,1},{21,5},{25,9},{29,13},{18,2},{... | collective-permute-start | bytes 393224 | tf_op jit(solution)/shard_map/ppermute | solution.py:179
  47.4 7.3 %collective-permute-done.7 = bf16[2,256,256]{2,1,0:T(8,128)(2,1)S(1)} collective-permute-done((bf16[2,256,256]{2,1,0:T(8,128)(2,1)S(1)}, bf16[2,256,256]{2,1,0:T(8,128)(2,1)S(1)}, u32[]{:S(2)}, u32[]{:S(2)}) %collective-permute-start.7) | collective-permute-done | bytes 262176 | tf_op jit(solution)/shard_map/ppermute | solution.py:179
  54.7 3.8 %collective-permute-done.8 = bf16[256,256]{1,0:T(8,128)(2,1)S(1)} collective-permute-done((bf16[256,256]{1,0:T(8,128)(2,1)S(1)}, bf16[256,256]{1,0:T(8,128)(2,1)S(1)}, u32[]{:S(2)}, u32[]{:S(2)}) %collective-permute-start.8) | collective-permute-done | bytes 131104 | tf_op jit(solution)/shard_map/ppermute | solution.py:179
  58.7 1.1 %collective-permute-start.13 = (bf16[2,768,128]{2,1,0:T(8,128)(2,1)S(1)}, bf16[2,768,128]{2,1,0:T(8,128)(2,1)S(1)}, u32[]{:S(2)}, u32[]{:S(2)}) collective-permute-start(bf16[2,768,128]{2,1,0:T(8,128)(2,1)S(1)} %collective-permute-done.12), channel_id=1, source_target_pairs={{0,2},{1,3},{2,0},{3,1},{4,6},{5,7},{6,4},{7,5},{8,10},{9,11},{10,... | collective-permute-start | bytes 1179656 | tf_op jit(solution)/shard_map/ppermute | solution.py:179
  59.8 10.0 %collective-permute-done.9.refs_1_ = bf16[2,256,256]{2,1,0:T(8,128)(2,1)S(1)} collective-permute-done((bf16[2,256,256]{2,1,0:T(8,128)(2,1)S(1)}, bf16[2,256,256]{2,1,0:T(8,128)(2,1)S(1)}, u32[]{:S(2)}, u32[]{:S(2)}) %collective-permute-start.9) | collective-permute-done | bytes 262176 | tf_op jit(solution)/shard_map/ppermute | solution.py:179
  69.8 3.0 %collective-permute-done.10.refs_2_ = bf16[2,256,256]{2,1,0:T(8,128)(2,1)S(1)} collective-permute-done((bf16[2,256,256]{2,1,0:T(8,128)(2,1)S(1)}, bf16[2,256,256]{2,1,0:T(8,128)(2,1)S(1)}, u32[]{:S(2)}, u32[]{:S(2)}) %collective-permute-start.10) | collective-permute-done | bytes 262176 | tf_op jit(solution)/shard_map/ppermute | solution.py:179
  73.4 11.2 %collective-permute-done.14 = bf16[2,256,384]{2,1,0:T(8,128)(2,1)S(1)} collective-permute-done((bf16[2,256,384]{2,1,0:T(8,128)(2,1)S(1)}, bf16[2,256,384]{2,1,0:T(8,128)(2,1)S(1)}, u32[]{:S(2)}, u32[]{:S(2)}) %collective-permute-start.14) | collective-permute-done | bytes 393248 | tf_op jit(solution)/shard_map/ppermute | solution.py:179
  84.7 1.6 %project.1 = (f32[384,256]{1,0:T(8,128)S(1)}, bf16[1,384,256]{2,1,0:T(8,128)(2,1)S(1)}) custom-call(s32[3]{0:T(128)S(1)} %pad_add_fusion.picks_ref, bf16[2,256,256]{2,1,0:T(8,128)(2,1)S(1)} %convert_element_type.11.refs_0_, bf16[2,256,256]{2,1,0:T(8,128)(2,1)S(1)} %collective-permute-done.9.refs_1_, ...), custom_call_target="tpu_custom_call" | custom-call | flops 32768 | bytes 32768 | tf_op jit(solution)/shard_map/project/pallas_call | solution.py:165
  88.2 4.6 %collective-permute-done.17 = bf16[384,256]{1,0:T(8,128)(2,1)S(1)} collective-permute-done((bf16[384,256]{1,0:T(8,128)(2,1)S(1)}, bf16[384,256]{1,0:T(8,128)(2,1)S(1)}, u32[]{:S(2)}, u32[]{:S(2)}) %collective-permute-start.17) | collective-permute-done | bytes 196640 | tf_op jit(solution)/shard_map/ppermute | solution.py:179
  92.9 1.0 %pad_maximum_fusion.1 = f32[384,512]{1,0:T(8,128)} fusion(f32[384,256]{1,0:T(8,128)S(1)} %get-tuple-element.60, f32[384,256]{1,0:T(8,128)S(1)} %get-tuple-element.59), kind=kLoop, calls=%fused_computation.1 | loop fusion | flops 196608 | bytes 1572864 | tf_op jit(solution)/shard_map/concatenate | solution.py:340
  (52 shorter events, 8.6 us)
Async XLA Ops:
  0.6 8.4 %copy-start.3 = (bf16[256,768]{1,0:T(8,128)(2,1)S(1)}, bf16[256,768]{1,0:T(8,128)(2,1)}, u32[]{:S(2)}) copy-start(bf16[256,768]{1,0:T(8,128)(2,1)} %g2.1) | copy-start | bytes 1179652
  0.6 8.4 %copy-start.2 = (bf16[256,768]{1,0:T(8,128)(2,1)S(1)}, bf16[256,768]{1,0:T(8,128)(2,1)}, u32[]{:S(2)}) copy-start(bf16[256,768]{1,0:T(8,128)(2,1)} %g1.1) | copy-start | bytes 1179652
  1.6 7.5 %copy-start = (bf16[256,768]{1,0:T(8,128)(2,1)S(1)}, bf16[256,768]{1,0:T(8,128)(2,1)}, u32[]{:S(2)}) copy-start(bf16[256,768]{1,0:T(8,128)(2,1)} %q1.1) | copy-start | bytes 1179652
  1.6 7.5 %copy-start.1 = (bf16[256,768]{1,0:T(8,128)(2,1)S(1)}, bf16[256,768]{1,0:T(8,128)(2,1)}, u32[]{:S(2)}) copy-start(bf16[256,768]{1,0:T(8,128)(2,1)} %q2.1) | copy-start | bytes 1179652
  2.7 8.1 %collective-permute-start = (bf16[256,256]{1,0:T(8,128)(2,1)S(1)}, bf16[256,256]{1,0:T(8,128)(2,1)S(1)}, u32[]{:S(2)}, u32[]{:S(2)}) collective-permute-start(bf16[256,256]{1,0:T(8,128)(2,1)S(1)} %get-tuple-element.74), channel_id=1, source_target_pairs={{0,4},{4,0},{8,12},{12,8},{16,20},{20,16},{24,28},{28,24},{1,5},{5... | collective-permute-start | bytes 393224 | tf_op jit(solution)/shard_map/ppermute | solution.py:179
  7.5 12.2 %collective-permute-start.3 = (bf16[128,768]{0,1:T(8,128)(2,1)}, bf16[128,768]{0,1:T(8,128)(2,1)}, u32[]{:S(2)}, u32[]{:S(2)}) collective-permute-start(bf16[128,768]{0,1:T(8,128)(2,1)} %copy.14), channel_id=1, source_target_pairs={{0,2},{1,3},{2,0},{3,1},{4,6},{5,7},{6,4},{7,5},{8,10},{9,11},{10,... | collective-permute-start | bytes 589832 | tf_op jit(solution)/shard_map/ppermute | solution.py:179
  10.2 17.2 %copy-start.4 = (s32[8]{0:T(128)S(1)}, s32[8]{0:T(128)}, u32[]{:S(2)}) copy-start(s32[8]{0:T(128)} %lens_ref.3) | copy-start | bytes 100
  10.2 26.5 %collective-permute-start.6 = (bf16[4,256,384]{2,1,0:T(8,128)(2,1)}, bf16[4,256,384]{2,1,0:T(8,128)(2,1)S(1)}, u32[]{:S(2)}, u32[]{:S(2)}) collective-permute-start(bf16[4,256,384]{2,1,0:T(8,128)(2,1)} %pad_maximum_fusion), channel_id=1, source_target_pairs={{0,4},{4,0},{8,12},{12,8},{16,20},{20,16},{24,28},{28,24},{1,5},{5... | collective-permute-start | bytes 2359304 | tf_op jit(solution)/shard_map/ppermute | solution.py:179
  11.5 11.2 %collective-permute-start.2 = (bf16[2,256,256]{2,1,0:T(8,128)(2,1)S(1)}, bf16[2,256,256]{2,1,0:T(8,128)(2,1)S(1)}, u32[]{:S(2)}, u32[]{:S(2)}) collective-permute-start(bf16[2,256,256]{2,1,0:T(8,128)(2,1)S(1)} %pad_maximum_fusion.4), channel_id=1, source_target_pairs={{0,8},{4,12},{8,16},{12,20},{16,24},{20,28},{1,9},{5,13},{9,17},{1... | collective-permute-start | bytes 786440 | tf_op jit(solution)/shard_map/ppermute | solution.py:179
  15.2 7.4 %collective-permute-start.1 = (bf16[256,256]{1,0:T(8,128)(2,1)}, bf16[256,256]{1,0:T(8,128)(2,1)S(1)}, u32[]{:S(2)}, u32[]{:S(2)}) collective-permute-start(bf16[256,256]{1,0:T(8,128)(2,1)} %get-tuple-element.57), channel_id=1, source_target_pairs={{0,16},{4,20},{8,24},{12,28},{1,17},{5,21},{9,25},{13,29},{2,18},{... | collective-permute-start | bytes 393224 | tf_op jit(solution)/shard_map/ppermute | solution.py:179
  22.7 14.1 %collective-permute-start.5 = (bf16[128,768]{0,1:T(8,128)(2,1)S(1)}, bf16[128,768]{0,1:T(8,128)(2,1)S(1)}, u32[]{:S(2)}, u32[]{:S(2)}) collective-permute-start(bf16[128,768]{0,1:T(8,128)(2,1)S(1)} %get-tuple-element.40), channel_id=1, source_target_pairs={{0,16},{1,24},{2,18},{3,26},{4,20},{5,28},{6,22},{7,30},{8,17},{9,... | collective-permute-start | bytes 589832 | tf_op jit(solution)/shard_map/ppermute | solution.py:179
  33.4 10.6 %collective-permute-start.4 = (bf16[128,768]{0,1:T(8,128)(2,1)S(1)}, bf16[128,768]{0,1:T(8,128)(2,1)S(1)}, u32[]{:S(2)}, u32[]{:S(2)}) collective-permute-start(bf16[128,768]{0,1:T(8,128)(2,1)S(1)} %get-tuple-element.39), channel_id=1, source_target_pairs={{0,0},{1,8},{2,2},{3,10},{4,4},{5,12},{6,6},{7,14},{8,1},{9,9},{10... | collective-permute-start | bytes 589832 | tf_op jit(solution)/shard_map/ppermute | solution.py:179
  42.5 12.2 %collective-permute-start.7 = (bf16[2,256,256]{2,1,0:T(8,128)(2,1)S(1)}, bf16[2,256,256]{2,1,0:T(8,128)(2,1)S(1)}, u32[]{:S(2)}, u32[]{:S(2)}) collective-permute-start(bf16[2,256,256]{2,1,0:T(8,128)(2,1)S(1)} %get-tuple-element.48), channel_id=1, source_target_pairs={{8,0},{12,4},{16,8},{20,12},{24,16},{28,20},{9,1},{13,5},{17,9},{2... | collective-permute-start | bytes 786440 | tf_op jit(solution)/shard_map/ppermute | solution.py:179
  44.0 28.8 %collective-permute-start.11 = (bf16[2,768,128]{2,1,0:T(8,128)(2,1)S(1)}, bf16[2,768,128]{2,1,0:T(8,128)(2,1)S(1)}, u32[]{:S(2)}, u32[]{:S(2)}) collective-permute-start(bf16[2,768,128]{2,1,0:T(8,128)(2,1)S(1)} %maximum_bitcast_fusion), channel_id=1, source_target_pairs={{0,2},{1,3},{2,0},{3,1},{4,6},{5,7},{6,4},{7,5},{8,10},{9,11},{10,... | collective-permute-start | bytes 1179656 | tf_op jit(solution)/shard_map/ppermute | solution.py:179
  44.6 14.1 %collective-permute-start.12 = (bf16[2,768,128]{2,1,0:T(8,128)(2,1)S(1)}, bf16[2,768,128]{2,1,0:T(8,128)(2,1)S(1)}, u32[]{:S(2)}, u32[]{:S(2)}) collective-permute-start(bf16[2,768,128]{2,1,0:T(8,128)(2,1)S(1)} %maximum_bitcast_fusion), channel_id=1, source_target_pairs={{0,4},{4,0},{8,12},{12,8},{16,20},{20,16},{24,28},{28,24},{1,5},{5... | collective-permute-start | bytes 1179656 | tf_op jit(solution)/shard_map/ppermute | solution.py:179
  46.1 12.4 %collective-permute-start.8 = (bf16[256,256]{1,0:T(8,128)(2,1)S(1)}, bf16[256,256]{1,0:T(8,128)(2,1)S(1)}, u32[]{:S(2)}, u32[]{:S(2)}) collective-permute-start(bf16[256,256]{1,0:T(8,128)(2,1)S(1)} %get-tuple-element.49), channel_id=1, source_target_pairs={{16,0},{20,4},{24,8},{28,12},{17,1},{21,5},{25,9},{29,13},{18,2},{... | collective-permute-start | bytes 393224 | tf_op jit(solution)/shard_map/ppermute | solution.py:179
  58.6 11.2 %collective-permute-start.9 = (bf16[2,256,256]{2,1,0:T(8,128)(2,1)S(1)}, bf16[2,256,256]{2,1,0:T(8,128)(2,1)S(1)}, u32[]{:S(2)}, u32[]{:S(2)}) collective-permute-start(bf16[2,256,256]{2,1,0:T(8,128)(2,1)S(1)} %convert_element_type.11.refs_0_), channel_id=1, source_target_pairs={{0,8},{4,12},{8,0},{12,4},{16,24},{20,28},{24,16},{28,20},{1,9},{5... | collective-permute-start | bytes 786440 | tf_op jit(solution)/shard_map/ppermute | solution.py:179
  58.6 14.1 %collective-permute-start.10 = (bf16[2,256,256]{2,1,0:T(8,128)(2,1)S(1)}, bf16[2,256,256]{2,1,0:T(8,128)(2,1)S(1)}, u32[]{:S(2)}, u32[]{:S(2)}) collective-permute-start(bf16[2,256,256]{2,1,0:T(8,128)(2,1)S(1)} %convert_element_type.11.refs_0_), channel_id=1, source_target_pairs={{0,16},{4,20},{8,24},{12,28},{16,0},{20,4},{24,8},{28,12},{1,17},{... | collective-permute-start | bytes 786440 | tf_op jit(solution)/shard_map/ppermute | solution.py:179
  58.7 14.2 %collective-permute-start.13 = (bf16[2,768,128]{2,1,0:T(8,128)(2,1)S(1)}, bf16[2,768,128]{2,1,0:T(8,128)(2,1)S(1)}, u32[]{:S(2)}, u32[]{:S(2)}) collective-permute-start(bf16[2,768,128]{2,1,0:T(8,128)(2,1)S(1)} %collective-permute-done.12), channel_id=1, source_target_pairs={{0,2},{1,3},{2,0},{3,1},{4,6},{5,7},{6,4},{7,5},{8,10},{9,11},{10,... | collective-permute-start | bytes 1179656 | tf_op jit(solution)/shard_map/ppermute | solution.py:179
  73.0 11.7 %collective-permute-start.16 = (bf16[8,768,128]{2,1,0:T(8,128)(2,1)S(1)}, bf16[8,768,128]{2,1,0:T(8,128)(2,1)S(1)}, u32[]{:S(2)}, u32[]{:S(2)}) collective-permute-start(bf16[8,768,128]{2,1,0:T(8,128)(2,1)S(1)} %constant_dynamic-update-slice_fusion.refs_4_), channel_id=1, source_target_pairs={{0,1},{1,0},{2,3},{3,2},{4,5},{5,4},{6,7},{7,6},{8,9},{9,8},{10,11... | collective-permute-start | bytes 4718600 | tf_op jit(solution)/shard_map/ppermute | solution.py:179
  73.1 11.5 %collective-permute-start.14 = (bf16[2,256,384]{2,1,0:T(8,128)(2,1)S(1)}, bf16[2,256,384]{2,1,0:T(8,128)(2,1)S(1)}, u32[]{:S(2)}, u32[]{:S(2)}) collective-permute-start(bf16[2,256,384]{2,1,0:T(8,128)(2,1)S(1)} %get-tuple-element.53), channel_id=1, source_target_pairs={{0,4},{4,0},{8,12},{12,8},{16,20},{20,16},{24,28},{28,24},{1,5},{5... | collective-permute-start | bytes 1179656 | tf_op jit(solution)/shard_map/ppermute | solution.py:179
  73.4 11.3 %collective-permute-start.15 = (bf16[2,256,256]{2,1,0:T(8,128)(2,1)S(1)}, bf16[2,256,256]{2,1,0:T(8,128)(2,1)S(1)}, u32[]{:S(2)}, u32[]{:S(2)}) collective-permute-start(bf16[2,256,256]{2,1,0:T(8,128)(2,1)S(1)} %collective-permute-done.10.refs_2_), channel_id=1, source_target_pairs={{0,8},{4,12},{8,0},{12,4},{16,24},{20,28},{24,16},{28,20},{1,9},{5... | collective-permute-start | bytes 786440 | tf_op jit(solution)/shard_map/ppermute | solution.py:179
  86.3 6.5 %collective-permute-start.17 = (bf16[384,256]{1,0:T(8,128)(2,1)S(1)}, bf16[384,256]{1,0:T(8,128)(2,1)S(1)}, u32[]{:S(2)}, u32[]{:S(2)}) collective-permute-start(bf16[384,256]{1,0:T(8,128)(2,1)S(1)} %bitcast.40), channel_id=1, source_target_pairs={{0,4},{4,0},{8,12},{12,8},{16,20},{20,16},{24,28},{28,24},{1,5},{5... | collective-permute-start | bytes 589832 | tf_op jit(solution)/shard_map/ppermute | solution.py:179

commit v3 on v2

--- a/solution.py
+++ b/solution.py
@@ -125,50 +125,15 @@
         ref[...] = scaled(acc_ref[i * rows:(i + 1) * rows, :]).astype(ref.dtype)
 
 
-def first_kernel(rows, group, here_ref, lens_ref, q1, q2, g1, g2, far, lifted, mine, got,
-                 made_ref, acc_ref, kv_ref, kt_ref, bias_ref, held_ref, sems):
-    lane = here_ref[0] % 2
-    ready = fetched((q1, q2, g1, g2), pl.ds(pl.multiple_of(lane * group * HD, HD), group * HD), held_ref, sems)
-    along, crosswise = lifted.at[0], lifted.at[1]
-    for i, pair in enumerate(((far, crosswise), (along, along), (crosswise, got), (mine, mine))):
-        chosen(lane, kv_ref, i, *pair)
-    attend(rows, group, here_ref[0], lens_ref, kv_ref, kt_ref, bias_ref, acc_ref, held_ref, made_ref, ready)
-
-
-def second_kernel(rows, group, here_ref, lens_ref, held_ref, far, lifted, mine, got, before_ref,
-                  made_ref, far_ref, pair_ref, own_ref, kv_ref, kt_ref, bias_ref, acc_ref):
-    lane = here_ref[0] % 2
-    along, crosswise = lifted.at[0], lifted.at[1]
-    for i, pair in enumerate(((along, far), (crosswise, crosswise), (mine, along), (got, got))):
-        chosen(lane, kv_ref, i, *pair)
-    attend(rows, group, here_ref[0] + 1 - 2 * lane, lens_ref, kv_ref, kt_ref, bias_ref, acc_ref, held_ref, made_ref, lambda: None)
-
-    def merged(even_ref, odd_ref):
-        block = lambda ref, i: ref[i * rows:(i + 1) * rows, :]
-        far_ref[...] = scaled(block(even_ref, 0)).astype(far_ref.dtype)
-        for i in range(2):
-            pair_ref[i] = scaled(block(even_ref, 1 + i) + block(odd_ref, i)).astype(pair_ref.dtype)
-        own_ref[0] = scaled(block(even_ref, 3) + block(odd_ref, 2))
-        own_ref[1] = scaled(block(odd_ref, 3))
-
-    @pl.when(lane == 0)
-    def _():
-        merged(before_ref, acc_ref)
-
-    @pl.when(lane == 1)
-    def _():
-        merged(acc_ref, before_ref)
-
-
-def called(kernel, name, operands, kinds, outs, scratch):
-    places = {"s": pltpu.SMEM, "v": pltpu.VMEM, "h": pltpu.HBM}
+def called(kernel, name, operands, kinds, outs, scratch, mebibytes=44):
+    places = {"s": pltpu.SMEM, "v": pltpu.VMEM, "h": pltpu.HBM, "a": pl.ANY}
     return pl.pallas_call(
         kernel,
         in_specs=[pl.BlockSpec(memory_space=places[k]) for k in kinds],
         out_specs=[pl.BlockSpec(memory_space=pltpu.VMEM)] * len(outs),
         out_shape=[jax.ShapeDtypeStruct(shape, dtype) for shape, dtype in outs],
         scratch_shapes=scratch,
-        compiler_params=pltpu.CompilerParams(vmem_limit_bytes=44 * 1024 * 1024),
+        compiler_params=pltpu.CompilerParams(vmem_limit_bytes=mebibytes * 1024 * 1024),
         cost_estimate=pl.CostEstimate(flops=1 << 15, bytes_accessed=1 << 15, transcendentals=0),
         name=name,
     )(*operands)
@@ -232,6 +197,41 @@
         functools.partial(project_kernel, len(blocks), len(hids) > 1), "project", [picks, *blocks, *hids],
         "s" + "v" * (len(blocks) + len(hids)),
         [((part, columns), jnp.float32), ((lanes - 1, part, columns), jnp.bfloat16)], [])
+
+
+def first_kernel(rows, group, here_ref, lens_ref, q1, q2, g1, g2, far, lifted, mine, got,
+                 made_ref, acc_ref, kv_ref, kt_ref, bias_ref, held_ref, sems):
+    lane = here_ref[0] % 2
+    ready = fetched((q1, q2, g1, g2), pl.ds(pl.multiple_of(lane * group * HD, HD), group * HD), held_ref, sems)
+    along, crosswise = lifted.at[0], lifted.at[1]
+    for i, pair in enumerate(((far, crosswise), (along, along), (crosswise, got), (mine, mine))):
+        chosen(lane, kv_ref, i, *pair)
+    attend(rows, group, here_ref[0], lens_ref, kv_ref, kt_ref, bias_ref, acc_ref, held_ref, made_ref, ready)
+
+
+def second_kernel(rows, group, here_ref, lens_ref, held_ref, far, lifted, mine, got, before_ref,
+                  made_ref, far_ref, pair_ref, own_ref, kv_ref, kt_ref, bias_ref, acc_ref):
+    lane = here_ref[0] % 2
+    along, crosswise = lifted.at[0], lifted.at[1]
+    for i, pair in enumerate(((along, far), (crosswise, crosswise), (mine, along), (got, got))):
+        chosen(lane, kv_ref, i, *pair)
+    attend(rows, group, here_ref[0] + 1 - 2 * lane, lens_ref, kv_ref, kt_ref, bias_ref, acc_ref, held_ref, made_ref, lambda: None)
+
+    def merged(even_ref, odd_ref):
+        block = lambda ref, i: ref[i * rows:(i + 1) * rows, :]
+        far_ref[...] = scaled(block(even_ref, 0)).astype(far_ref.dtype)
+        for i in range(2):
+            pair_ref[i] = scaled(block(even_ref, 1 + i) + block(odd_ref, i)).astype(pair_ref.dtype)
+        own_ref[0] = scaled(block(even_ref, 3) + block(odd_ref, 2))
+        own_ref[1] = scaled(block(odd_ref, 3))
+
+    @pl.when(lane == 0)
+    def _():
+        merged(before_ref, acc_ref)
+
+    @pl.when(lane == 1)
+    def _():
+        merged(acc_ref, before_ref)
 
 
 def general(place, line, lane, head, heads, tokens, lanes, kv_heads, lens, arrays, stacked, hidden_states):
@@ -295,20 +295,19 @@
             return (((z // 2) ^ flip) * 2 + c) * lanes * heads + (t % lanes) * heads + (h // 2) * 2 + z % 2
         return place_of
 
+    y = head // 2
+    half = rows // 2
     given = jnp.where(even, stacked[1], stacked[0])
     mine = jnp.where(even, after(stacked[0], given), stacked[1])
     got = over(given)
+    asked = over(jnp.stack([jnp.where(even, a[:, wide:], a[:, :wide]) for a in (after(x, given) for x in arrays)]))
     risen = jnp.stack([mine, got])
     lifted = up(risen, 1)
     far = up(jnp.where(even, got, mine), 2)
-    asked = over(jnp.stack([jnp.where(even, a[:, wide:], a[:, :wide]) for a in (after(x, given) for x in arrays)]))
-    y = head // 2
-    half = rows // 2
-    kept, lent = (lax.dynamic_slice_in_dim(hidden_states, at * half, half, 0) for at in (y, 1 - y))
+    kept, lent = (lax.dynamic_slice_in_dim(after(hidden_states, given), at * half, half, 0) for at in (y, 1 - y))
     lent = moved(lent, "head", lambda h: h ^ 2)
     own_line = (line // 2) == y
     afar = moved(after(jnp.where(own_line, lent, kept), lifted, far), both, crossed(1))
-
     window = [far, lifted, mine, got]
     keys = (REACH + 1) * rows
     made, sums = called(
@@ -322,21 +321,20 @@
         [((2, rows, wide), jnp.bfloat16), ((rows, 2 * HD), jnp.bfloat16), ((2, rows, 2 * HD), jnp.bfloat16),
          ((2, rows, 2 * HD), jnp.float32)],
         attend_scratch(rows) + [pltpu.VMEM((keys, 2 * HD), jnp.float32)])
-
     one, two = down(nearer, 1), down(farther, 2)
+    sent = over(made_other)
     hops = jnp.swapaxes(jnp.stack([nearby, after(afar, own)]), 1, 2)
-    beside = over(hops)
-    hids = [hops, moved(hops, "head", lambda h: h ^ 2), beside, moved(beside, "head", lambda h: h ^ 2)]
+    beside, upright = over(hops), moved(hops, "head", lambda h: h ^ 2)
+    skew = moved(after(beside, one), "head", lambda h: h ^ 2)
     total = (own + one.astype(jnp.float32)).at[1].add(two.astype(jnp.float32)).astype(jnp.bfloat16)
     across = moved(total, "tok", lambda t: t ^ (2 * lanes))
-    blocks = [total, moved(total, "tok", lambda t: t ^ lanes), across, moved(across, "tok", lambda t: t ^ lanes)]
-    sent = over(after(made_other, total))
-    hids = jnp.concatenate([after(hids[0], *blocks[1:3])] + hids[1:], axis=0)
-    firsts, seconds = (jnp.concatenate(mine_and_other(after(made[l], hids), sent[l]), axis=1) for l in range(2))
-
+    j1 = moved(total, "tok", lambda t: t ^ lanes)
+    blocks = [total, j1, across, moved(after(across, j1), "tok", lambda t: t ^ lanes)]
+    hids = jnp.concatenate([after(hops, j1, across, sent), upright, beside, skew], axis=0)
     picks = jnp.stack([line, head, lane]).astype(jnp.int32)
     kept, away = project(picks, [hids, moved(hids, "head", lambda h: h ^ 1)], blocks, lanes)
     came = over(away[0]).astype(jnp.float32)
+    firsts, seconds = (jnp.concatenate(mine_and_other(made[l], sent[l]), axis=1) for l in range(2))
     return (firsts, seconds, jnp.concatenate(mine_and_other(kept, came), axis=1))
 
 
@@ -346,8 +344,7 @@
     lanes = tokens // heads
     here, head = lax.axis_index("tok"), lax.axis_index("head")
     arrays = (queries_first, queries_second, grads_first, grads_second)
-    stacked = [jnp.concatenate([key_states[:, c * HD:(c + 1) * HD], value_states[:, c * HD:(c + 1) * HD]], axis=1)
-               for c in range(kv_heads)]
+    stacked = [jnp.concatenate([x[:, c * HD:(c + 1) * HD] for x in (key_states, value_states)], axis=1) for c in range(kv_heads)]
     plan = paired if (lanes, heads, kv_heads, REACH) == (2, 4, 2, 3) else general
     return plan(here.reshape(1).astype(jnp.int32), here // lanes, here % lanes, head, heads, tokens, lanes, kv_heads,
                 doc_lengths, arrays, stacked, hidden_states)

time: 94.2 us -> 90.3 us (0.959)
  waiting for transfers between devices: 44.4 us -> 38.4 us
  starting transfers between devices: 25.2 us -> 27.5 us
    ppermute x18, waiting for transfers between devices: 44.4 us -> 38.4 us  [moved(): lax.ppermute(value, axis, [(i, j) for i, j in pairs if j is not None])]
    ppermute x18, starting transfers between devices: 25.2 us -> 27.5 us  [moved(): lax.ppermute(value, axis, [(i, j) for i, j in pairs if j is not None])]
    optimization_barrier x0 -> x1, local copies, waits for them, and re-layouts: none -> 1.16 us  [after(): return lax.optimization_barrier((value,) + earlier)[0]]
    unnamed x15 -> x13, local copies, waits for them, and re-layouts: 1.14 us -> 0.16 us
  transfers between devices with their start and end apart: 18 -> 18, of which waited for: 8 -> 9; matrix products, arithmetic and copies ran while one was open for 7% -> 7% of each run, Pallas kernels for 13% -> 13%
where the time goes in v3:
time: 90.3 us; the launch traced here: 90 us
  waiting for transfers between devices  38.4 us (43%)
  starting transfers between devices  27.5 us (30%)
  Pallas kernels  13.3 us (15%)
  other arithmetic  5.86 us (6%)
  local copies, waits for them, and re-layouts  3.98 us (4%)
  between operations  0.99 us (1%)
    ppermute x18, waiting for transfers between devices, moved(): lax.ppermute(value, axis, [(i, j) for i, j in pairs if j is not None])  38.4 us
    ppermute x18, starting transfers between devices, moved(): lax.ppermute(value, axis, [(i, j) for i, j in pairs if j is not None])  27.5 us
    pallas_call x3, Pallas kernels, called(): pl.pallas_call(kernel, in_specs=[pl.BlockSpec(memory_space=places[k]) for...  13.3 us
    slice x2, local copies, waits for them, and re-layouts, body(): x[:, c * HD:(c + 1) * HD]  1.9 us
  transfers between devices with their start and end apart: 18, of which 9 were waited for; matrix products, arithmetic and copies ran while one was open for 7% of the time, Pallas kernels for 13%

profile of v3, /device:TPU:0, one launch (start us, length us, event | category | flops | bytes accessed | tf_op | source)
XLA Modules:
  0.0 90.0 jit_solution(15156599454082738978)
XLA Ops:
  2.7 3.0 %collective-permute-start = (bf16[256,256]{1,0:T(8,128)(2,1)S(1)}, bf16[256,256]{1,0:T(8,128)(2,1)S(1)}, u32[]{:S(2)}, u32[]{:S(2)}) collective-permute-start(bf16[256,256]{1,0:T(8,128)(2,1)S(1)} %get-tuple-element.68), channel_id=1, source_target_pairs={{0,4},{4,0},{8,12},{12,8},{16,20},{20,16},{24,28},{28,24},{1,5},{5... | collective-permute-start | bytes 393224 | tf_op jit(solution)/shard_map/ppermute | solution.py:144
  5.7 1.2 %copy.11 = bf16[256,768]{0,1:T(8,128)(2,1)S(1)} copy(bf16[256,768]{1,0:T(8,128)(2,1)} %param.17) | data formatting | bytes 786432 | tf_op jit(solution)/shard_map/optimization_barrier | solution.py:148
  7.5 1.5 %collective-permute-start.4 = (bf16[128,768]{0,1:T(8,128)(2,1)}, bf16[128,768]{0,1:T(8,128)(2,1)}, u32[]{:S(2)}, u32[]{:S(2)}) collective-permute-start(bf16[128,768]{0,1:T(8,128)(2,1)} %constant_dynamic-slice_fusion), channel_id=1, source_target_pairs={{0,2},{1,3},{2,0},{3,1},{4,6},{5,7},{6,4},{7,5},{8,10},{9,11},{10,... | collective-permute-start | bytes 589832 | tf_op jit(solution)/shard_map/ppermute | solution.py:144
  11.5 3.5 %collective-permute-start.2 = (bf16[2,256,256]{2,1,0:T(8,128)(2,1)S(1)}, bf16[2,256,256]{2,1,0:T(8,128)(2,1)S(1)}, u32[]{:S(2)}, u32[]{:S(2)}) collective-permute-start(bf16[2,256,256]{2,1,0:T(8,128)(2,1)S(1)} %pad_maximum_fusion.4), channel_id=1, source_target_pairs={{0,8},{4,12},{8,16},{12,20},{16,24},{20,28},{1,9},{5,13},{9,17},{1... | collective-permute-start | bytes 786440 | tf_op jit(solution)/shard_map/ppermute | solution.py:144
  15.0 4.5 %collective-permute-start.1 = (bf16[256,256]{1,0:T(8,128)(2,1)}, bf16[256,256]{1,0:T(8,128)(2,1)S(1)}, u32[]{:S(2)}, u32[]{:S(2)}) collective-permute-start(bf16[256,256]{1,0:T(8,128)(2,1)} %get-tuple-element.57), channel_id=1, source_target_pairs={{0,16},{4,20},{8,24},{12,28},{1,17},{5,21},{9,25},{13,29},{2,18},{... | collective-permute-start | bytes 393224 | tf_op jit(solution)/shard_map/ppermute | solution.py:144
  19.6 1.0 %broadcast_select_fusion = (bf16[128,768]{0,1:T(8,128)(2,1)S(1)}, bf16[128,768]{0,1:T(8,128)(2,1)S(1)}) fusion(bf16[128,768]{0,1:T(8,128)(2,1)} %collective-permute-done.4, pred[]{:T(512)S(6)} %eq.9, bf16[256,768]{0,1:T(8,128)(2,1)S(1)} %copy.11, s32[]{:T(128)S(6)} %select_n.129), kind=kLoop, calls=%fused_computation.19 | loop fusion | flops 196608 | bytes 786437 | tf_op jit(solution)/shard_map/jit(_where)/select_n | solution.py:317
  20.6 2.1 %collective-permute-done.1.far = bf16[256,256]{1,0:T(8,128)(2,1)S(1)} collective-permute-done((bf16[256,256]{1,0:T(8,128)(2,1)}, bf16[256,256]{1,0:T(8,128)(2,1)S(1)}, u32[]{:S(2)}, u32[]{:S(2)}) %collective-permute-start.1) | collective-permute-done | bytes 131104 | tf_op jit(solution)/shard_map/ppermute | solution.py:144
  22.7 4.7 %collective-permute-start.5 = (bf16[128,768]{0,1:T(8,128)(2,1)S(1)}, bf16[128,768]{0,1:T(8,128)(2,1)S(1)}, u32[]{:S(2)}, u32[]{:S(2)}) collective-permute-start(bf16[128,768]{0,1:T(8,128)(2,1)S(1)} %get-tuple-element.44), channel_id=1, source_target_pairs={{0,16},{1,24},{2,18},{3,26},{4,20},{5,28},{6,22},{7,30},{8,17},{9,... | collective-permute-start | bytes 589832 | tf_op jit(solution)/shard_map/ppermute | solution.py:144
  27.4 6.0 %attend_own.1 = (bf16[2,256,384]{2,1,0:T(8,128)(2,1)S(1)}, f32[1024,256]{1,0:T(8,128)S(1)}) custom-call(s32[1]{0:T(128)} %bitcast.here_ref, s32[8]{0:T(128)S(1)} %copy-done.4, bf16[256,768]{1,0:T(8,128)(2,1)S(1)} %copy-done.3, bf16[256,768]{1,0:T(8,128)(2,1)S(1)} %copy-done.2, bf16[256,768]{1,0:T(8,128)(2,1)S(1)} %copy-done.1, bf16[256,768]{1,0:T(8,128)(2,1)S(1)} %copy-done, ...), custom_call_target="tpu_custom_call" | custom-call | flops 32768 | bytes 32768 | tf_op jit(solution)/shard_map/attend_own/pallas_call | solution.py:130
  34.0 2.7 %collective-permute-done.5 = bf16[128,768]{0,1:T(8,128)(2,1)S(1)} collective-permute-done((bf16[128,768]{0,1:T(8,128)(2,1)S(1)}, bf16[128,768]{0,1:T(8,128)(2,1)S(1)}, u32[]{:S(2)}, u32[]{:S(2)}) %collective-permute-start.5) | collective-permute-done | bytes 196640 | tf_op jit(solution)/shard_map/ppermute | solution.py:144
  36.7 5.8 %attend_other.1 = (bf16[2,256,384]{2,1,0:T(8,128)(2,1)S(1)}, bf16[256,256]{1,0:T(8,128)(2,1)S(1)}, bf16[2,256,256]{2,1,0:T(8,128)(2,1)S(1)}, f32[2,256,256]{2,1,0:T(8,128)S(1)}) custom-call(s32[1]{0:T(128)} %bitcast.here_ref, s32[8]{0:T(128)S(1)} %copy-done.4, bf16[4,256,384]{2,1,0:T(8,128)(2,1)S(1)} %collective-permute-done.3.held_ref, ...), custom_call_target="tpu_custom_call" | custom-call | flops 32768 | bytes 32768 | tf_op jit(solution)/shard_map/attend_other/pallas_call | solution.py:130
  42.5 1.5 %collective-permute-start.7 = (bf16[2,256,256]{2,1,0:T(8,128)(2,1)S(1)}, bf16[2,256,256]{2,1,0:T(8,128)(2,1)S(1)}, u32[]{:S(2)}, u32[]{:S(2)}) collective-permute-start(bf16[2,256,256]{2,1,0:T(8,128)(2,1)S(1)} %get-tuple-element.48), channel_id=1, source_target_pairs={{8,0},{12,4},{16,8},{20,12},{24,16},{28,20},{9,1},{13,5},{17,9},{2... | collective-permute-start | bytes 786440 | tf_op jit(solution)/shard_map/ppermute | solution.py:144
  44.0 1.6 %collective-permute-start.14 = (bf16[2,768,128]{2,1,0:T(8,128)(2,1)S(1)}, bf16[2,768,128]{2,1,0:T(8,128)(2,1)S(1)}, u32[]{:S(2)}, u32[]{:S(2)}) collective-permute-start(bf16[2,768,128]{2,1,0:T(8,128)(2,1)S(1)} %maximum_bitcast_fusion), channel_id=1, source_target_pairs={{0,4},{4,0},{8,12},{12,8},{16,20},{20,16},{24,28},{28,24},{1,5},{5... | collective-permute-start | bytes 1179656 | tf_op jit(solution)/shard_map/ppermute | solution.py:144
  46.1 1.3 %collective-permute-start.8 = (bf16[256,256]{1,0:T(8,128)(2,1)S(1)}, bf16[256,256]{1,0:T(8,128)(2,1)S(1)}, u32[]{:S(2)}, u32[]{:S(2)}) collective-permute-start(bf16[256,256]{1,0:T(8,128)(2,1)S(1)} %get-tuple-element.49), channel_id=1, source_target_pairs={{16,0},{20,4},{24,8},{28,12},{17,1},{21,5},{25,9},{29,13},{18,2},{... | collective-permute-start | bytes 393224 | tf_op jit(solution)/shard_map/ppermute | solution.py:144
  48.0 6.6 %collective-permute-done.7 = bf16[2,256,256]{2,1,0:T(8,128)(2,1)S(1)} collective-permute-done((bf16[2,256,256]{2,1,0:T(8,128)(2,1)S(1)}, bf16[2,256,256]{2,1,0:T(8,128)(2,1)S(1)}, u32[]{:S(2)}, u32[]{:S(2)}) %collective-permute-start.7) | collective-permute-done | bytes 262176 | tf_op jit(solution)/shard_map/ppermute | solution.py:144
  54.7 3.8 %collective-permute-done.8 = bf16[256,256]{1,0:T(8,128)(2,1)S(1)} collective-permute-done((bf16[256,256]{1,0:T(8,128)(2,1)S(1)}, bf16[256,256]{1,0:T(8,128)(2,1)S(1)}, u32[]{:S(2)}, u32[]{:S(2)}) %collective-permute-start.8) | collective-permute-done | bytes 131104 | tf_op jit(solution)/shard_map/ppermute | solution.py:144
  58.7 1.5 %collective-permute-start.15 = (bf16[2,768,128]{2,1,0:T(8,128)(2,1)S(1)}, bf16[2,768,128]{2,1,0:T(8,128)(2,1)S(1)}, u32[]{:S(2)}, u32[]{:S(2)}) collective-permute-start(bf16[2,768,128]{2,1,0:T(8,128)(2,1)S(1)} %collective-permute-done.14), channel_id=1, source_target_pairs={{0,2},{1,3},{2,0},{3,1},{4,6},{5,7},{6,4},{7,5},{8,10},{9,11},{10,... | collective-permute-start | bytes 1179656 | tf_op jit(solution)/shard_map/ppermute | solution.py:144
  60.2 4.2 %collective-permute-done.6 = bf16[2,256,384]{2,1,0:T(8,128)(2,1)S(1)} collective-permute-done((bf16[2,256,384]{2,1,0:T(8,128)(2,1)S(1)}, bf16[2,256,384]{2,1,0:T(8,128)(2,1)S(1)}, u32[]{:S(2)}, u32[]{:S(2)}) %collective-permute-start.6) | collective-permute-done | bytes 393248 | tf_op jit(solution)/shard_map/ppermute | solution.py:144
  64.5 5.6 %collective-permute-done.10.refs_2_ = bf16[2,256,256]{2,1,0:T(8,128)(2,1)S(1)} collective-permute-done((bf16[2,256,256]{2,1,0:T(8,128)(2,1)S(1)}, bf16[2,256,256]{2,1,0:T(8,128)(2,1)S(1)}, u32[]{:S(2)}, u32[]{:S(2)}) %collective-permute-start.10) | collective-permute-done | bytes 262176 | tf_op jit(solution)/shard_map/ppermute | solution.py:144
  70.1 1.7 %collective-permute-done.9.refs_1_ = bf16[2,256,256]{2,1,0:T(8,128)(2,1)S(1)} collective-permute-done((bf16[2,256,256]{2,1,0:T(8,128)(2,1)S(1)}, bf16[2,256,256]{2,1,0:T(8,128)(2,1)S(1)}, u32[]{:S(2)}, u32[]{:S(2)}) %collective-permute-start.9) | collective-permute-done | bytes 262176 | tf_op jit(solution)/shard_map/ppermute | solution.py:144
  72.6 8.2 %collective-permute-done.11.refs_3_ = bf16[2,256,256]{2,1,0:T(8,128)(2,1)S(1)} collective-permute-done((bf16[2,256,256]{2,1,0:T(8,128)(2,1)S(1)}, bf16[2,256,256]{2,1,0:T(8,128)(2,1)S(1)}, u32[]{:S(2)}, u32[]{:S(2)}) %collective-permute-start.11) | collective-permute-done | bytes 262176 | tf_op jit(solution)/shard_map/ppermute | solution.py:144
  80.8 1.6 %project.1 = (f32[384,256]{1,0:T(8,128)S(1)}, bf16[1,384,256]{2,1,0:T(8,128)(2,1)S(1)}) custom-call(s32[3]{0:T(128)S(1)} %pad_add_fusion.picks_ref, bf16[2,256,256]{2,1,0:T(8,128)(2,1)S(1)} %convert_element_type.11.refs_0_, bf16[2,256,256]{2,1,0:T(8,128)(2,1)S(1)} %collective-permute-done.9.refs_1_, ...), custom_call_target="tpu_custom_call" | custom-call | flops 32768 | bytes 32768 | tf_op jit(solution)/shard_map/project/pallas_call | solution.py:130
  82.4 1.6 %collective-permute-start.17 = (bf16[384,256]{1,0:T(8,128)(2,1)S(1)}, bf16[384,256]{1,0:T(8,128)(2,1)S(1)}, u32[]{:S(2)}, u32[]{:S(2)}) collective-permute-start(bf16[384,256]{1,0:T(8,128)(2,1)S(1)} %bitcast.32), channel_id=1, source_target_pairs={{0,4},{4,0},{8,12},{12,8},{16,20},{20,16},{24,28},{28,24},{1,5},{5... | collective-permute-start | bytes 589832 | tf_op jit(solution)/shard_map/ppermute | solution.py:144
  85.6 3.4 %collective-permute-done.17 = bf16[384,256]{1,0:T(8,128)(2,1)S(1)} collective-permute-done((bf16[384,256]{1,0:T(8,128)(2,1)S(1)}, bf16[384,256]{1,0:T(8,128)(2,1)S(1)}, u32[]{:S(2)}, u32[]{:S(2)}) %collective-permute-start.17) | collective-permute-done | bytes 196640 | tf_op jit(solution)/shard_map/ppermute | solution.py:144
  (50 shorter events, 10.5 us)
Async XLA Ops:
  0.6 8.4 %copy-start.3 = (bf16[256,768]{1,0:T(8,128)(2,1)S(1)}, bf16[256,768]{1,0:T(8,128)(2,1)}, u32[]{:S(2)}) copy-start(bf16[256,768]{1,0:T(8,128)(2,1)} %q1.1) | copy-start | bytes 1179652
  0.6 8.4 %copy-start.2 = (bf16[256,768]{1,0:T(8,128)(2,1)S(1)}, bf16[256,768]{1,0:T(8,128)(2,1)}, u32[]{:S(2)}) copy-start(bf16[256,768]{1,0:T(8,128)(2,1)} %q2.1) | copy-start | bytes 1179652
  1.6 7.5 %copy-start = (bf16[256,768]{1,0:T(8,128)(2,1)S(1)}, bf16[256,768]{1,0:T(8,128)(2,1)}, u32[]{:S(2)}) copy-start(bf16[256,768]{1,0:T(8,128)(2,1)} %g2.1) | copy-start | bytes 1179652
  1.6 7.5 %copy-start.1 = (bf16[256,768]{1,0:T(8,128)(2,1)S(1)}, bf16[256,768]{1,0:T(8,128)(2,1)}, u32[]{:S(2)}) copy-start(bf16[256,768]{1,0:T(8,128)(2,1)} %g1.1) | copy-start | bytes 1179652
  2.7 8.1 %collective-permute-start = (bf16[256,256]{1,0:T(8,128)(2,1)S(1)}, bf16[256,256]{1,0:T(8,128)(2,1)S(1)}, u32[]{:S(2)}, u32[]{:S(2)}) collective-permute-start(bf16[256,256]{1,0:T(8,128)(2,1)S(1)} %get-tuple-element.68), channel_id=1, source_target_pairs={{0,4},{4,0},{8,12},{12,8},{16,20},{20,16},{24,28},{28,24},{1,5},{5... | collective-permute-start | bytes 393224 | tf_op jit(solution)/shard_map/ppermute | solution.py:144
  7.5 12.0 %collective-permute-start.4 = (bf16[128,768]{0,1:T(8,128)(2,1)}, bf16[128,768]{0,1:T(8,128)(2,1)}, u32[]{:S(2)}, u32[]{:S(2)}) collective-permute-start(bf16[128,768]{0,1:T(8,128)(2,1)} %constant_dynamic-slice_fusion), channel_id=1, source_target_pairs={{0,2},{1,3},{2,0},{3,1},{4,6},{5,7},{6,4},{7,5},{8,10},{9,11},{10,... | collective-permute-start | bytes 589832 | tf_op jit(solution)/shard_map/ppermute | solution.py:144
  9.2 18.2 %copy-start.4 = (s32[8]{0:T(128)S(1)}, s32[8]{0:T(128)}, u32[]{:S(2)}) copy-start(s32[8]{0:T(128)} %lens_ref.3) | copy-start | bytes 100
  10.2 26.5 %collective-permute-start.3 = (bf16[4,256,384]{2,1,0:T(8,128)(2,1)}, bf16[4,256,384]{2,1,0:T(8,128)(2,1)S(1)}, u32[]{:S(2)}, u32[]{:S(2)}) collective-permute-start(bf16[4,256,384]{2,1,0:T(8,128)(2,1)} %pad_maximum_fusion), channel_id=1, source_target_pairs={{0,4},{4,0},{8,12},{12,8},{16,20},{20,16},{24,28},{28,24},{1,5},{5... | collective-permute-start | bytes 2359304 | tf_op jit(solution)/shard_map/ppermute | solution.py:144
  11.5 11.2 %collective-permute-start.2 = (bf16[2,256,256]{2,1,0:T(8,128)(2,1)S(1)}, bf16[2,256,256]{2,1,0:T(8,128)(2,1)S(1)}, u32[]{:S(2)}, u32[]{:S(2)}) collective-permute-start(bf16[2,256,256]{2,1,0:T(8,128)(2,1)S(1)} %pad_maximum_fusion.4), channel_id=1, source_target_pairs={{0,8},{4,12},{8,16},{12,20},{16,24},{20,28},{1,9},{5,13},{9,17},{1... | collective-permute-start | bytes 786440 | tf_op jit(solution)/shard_map/ppermute | solution.py:144
  15.0 7.6 %collective-permute-start.1 = (bf16[256,256]{1,0:T(8,128)(2,1)}, bf16[256,256]{1,0:T(8,128)(2,1)S(1)}, u32[]{:S(2)}, u32[]{:S(2)}) collective-permute-start(bf16[256,256]{1,0:T(8,128)(2,1)} %get-tuple-element.57), channel_id=1, source_target_pairs={{0,16},{4,20},{8,24},{12,28},{1,17},{5,21},{9,25},{13,29},{2,18},{... | collective-permute-start | bytes 393224 | tf_op jit(solution)/shard_map/ppermute | solution.py:144
  22.7 14.1 %collective-permute-start.5 = (bf16[128,768]{0,1:T(8,128)(2,1)S(1)}, bf16[128,768]{0,1:T(8,128)(2,1)S(1)}, u32[]{:S(2)}, u32[]{:S(2)}) collective-permute-start(bf16[128,768]{0,1:T(8,128)(2,1)S(1)} %get-tuple-element.44), channel_id=1, source_target_pairs={{0,16},{1,24},{2,18},{3,26},{4,20},{5,28},{6,22},{7,30},{8,17},{9,... | collective-permute-start | bytes 589832 | tf_op jit(solution)/shard_map/ppermute | solution.py:144
  33.4 10.6 %collective-permute-start.12 = (bf16[128,768]{0,1:T(8,128)(2,1)S(1)}, bf16[128,768]{0,1:T(8,128)(2,1)S(1)}, u32[]{:S(2)}, u32[]{:S(2)}) collective-permute-start(bf16[128,768]{0,1:T(8,128)(2,1)S(1)} %get-tuple-element.51), channel_id=1, source_target_pairs={{0,0},{1,8},{2,2},{3,10},{4,4},{5,12},{6,6},{7,14},{8,1},{9,9},{10... | collective-permute-start | bytes 589832 | tf_op jit(solution)/shard_map/ppermute | solution.py:144
  42.5 12.1 %collective-permute-start.7 = (bf16[2,256,256]{2,1,0:T(8,128)(2,1)S(1)}, bf16[2,256,256]{2,1,0:T(8,128)(2,1)S(1)}, u32[]{:S(2)}, u32[]{:S(2)}) collective-permute-start(bf16[2,256,256]{2,1,0:T(8,128)(2,1)S(1)} %get-tuple-element.48), channel_id=1, source_target_pairs={{8,0},{12,4},{16,8},{20,12},{24,16},{28,20},{9,1},{13,5},{17,9},{2... | collective-permute-start | bytes 786440 | tf_op jit(solution)/shard_map/ppermute | solution.py:144
  44.0 14.7 %collective-permute-start.14 = (bf16[2,768,128]{2,1,0:T(8,128)(2,1)S(1)}, bf16[2,768,128]{2,1,0:T(8,128)(2,1)S(1)}, u32[]{:S(2)}, u32[]{:S(2)}) collective-permute-start(bf16[2,768,128]{2,1,0:T(8,128)(2,1)S(1)} %maximum_bitcast_fusion), channel_id=1, source_target_pairs={{0,4},{4,0},{8,12},{12,8},{16,20},{20,16},{24,28},{28,24},{1,5},{5... | collective-permute-start | bytes 1179656 | tf_op jit(solution)/shard_map/ppermute | solution.py:144
  45.6 26.2 %collective-permute-start.13 = (bf16[2,768,128]{2,1,0:T(8,128)(2,1)S(1)}, bf16[2,768,128]{2,1,0:T(8,128)(2,1)S(1)}, u32[]{:S(2)}, u32[]{:S(2)}) collective-permute-start(bf16[2,768,128]{2,1,0:T(8,128)(2,1)S(1)} %maximum_bitcast_fusion), channel_id=1, source_target_pairs={{0,2},{1,3},{2,0},{3,1},{4,6},{5,7},{6,4},{7,5},{8,10},{9,11},{10,... | collective-permute-start | bytes 1179656 | tf_op jit(solution)/shard_map/ppermute | solution.py:144
  46.1 12.4 %collective-permute-start.8 = (bf16[256,256]{1,0:T(8,128)(2,1)S(1)}, bf16[256,256]{1,0:T(8,128)(2,1)S(1)}, u32[]{:S(2)}, u32[]{:S(2)}) collective-permute-start(bf16[256,256]{1,0:T(8,128)(2,1)S(1)} %get-tuple-element.49), channel_id=1, source_target_pairs={{16,0},{20,4},{24,8},{28,12},{17,1},{21,5},{25,9},{29,13},{18,2},{... | collective-permute-start | bytes 393224 | tf_op jit(solution)/shard_map/ppermute | solution.py:144
  47.4 17.1 %collective-permute-start.6 = (bf16[2,256,384]{2,1,0:T(8,128)(2,1)S(1)}, bf16[2,256,384]{2,1,0:T(8,128)(2,1)S(1)}, u32[]{:S(2)}, u32[]{:S(2)}) collective-permute-start(bf16[2,256,384]{2,1,0:T(8,128)(2,1)S(1)} %get-tuple-element.46), channel_id=1, source_target_pairs={{0,4},{4,0},{8,12},{12,8},{16,20},{20,16},{24,28},{28,24},{1,5},{5... | collective-permute-start | bytes 1179656 | tf_op jit(solution)/shard_map/ppermute | solution.py:144
  58.5 11.5 %collective-permute-start.10 = (bf16[2,256,256]{2,1,0:T(8,128)(2,1)S(1)}, bf16[2,256,256]{2,1,0:T(8,128)(2,1)S(1)}, u32[]{:S(2)}, u32[]{:S(2)}) collective-permute-start(bf16[2,256,256]{2,1,0:T(8,128)(2,1)S(1)} %convert_element_type.11.refs_0_), channel_id=1, source_target_pairs={{0,16},{4,20},{8,24},{12,28},{16,0},{20,4},{24,8},{28,12},{1,17},{... | collective-permute-start | bytes 786440 | tf_op jit(solution)/shard_map/ppermute | solution.py:144
  58.6 13.2 %collective-permute-start.9 = (bf16[2,256,256]{2,1,0:T(8,128)(2,1)S(1)}, bf16[2,256,256]{2,1,0:T(8,128)(2,1)S(1)}, u32[]{:S(2)}, u32[]{:S(2)}) collective-permute-start(bf16[2,256,256]{2,1,0:T(8,128)(2,1)S(1)} %convert_element_type.11.refs_0_), channel_id=1, source_target_pairs={{0,8},{4,12},{8,0},{12,4},{16,24},{20,28},{24,16},{28,20},{1,9},{5... | collective-permute-start | bytes 786440 | tf_op jit(solution)/shard_map/ppermute | solution.py:144
  58.7 13.3 %collective-permute-start.15 = (bf16[2,768,128]{2,1,0:T(8,128)(2,1)S(1)}, bf16[2,768,128]{2,1,0:T(8,128)(2,1)S(1)}, u32[]{:S(2)}, u32[]{:S(2)}) collective-permute-start(bf16[2,768,128]{2,1,0:T(8,128)(2,1)S(1)} %collective-permute-done.14), channel_id=1, source_target_pairs={{0,2},{1,3},{2,0},{3,1},{4,6},{5,7},{6,4},{7,5},{8,10},{9,11},{10,... | collective-permute-start | bytes 1179656 | tf_op jit(solution)/shard_map/ppermute | solution.py:144
  72.0 8.8 %collective-permute-start.16 = (bf16[8,768,128]{2,1,0:T(8,128)(2,1)S(1)}, bf16[8,768,128]{2,1,0:T(8,128)(2,1)S(1)}, u32[]{:S(2)}, u32[]{:S(2)}) collective-permute-start(bf16[8,768,128]{2,1,0:T(8,128)(2,1)S(1)} %constant_dynamic-update-slice_fusion.refs_4_), channel_id=1, source_target_pairs={{0,1},{1,0},{2,3},{3,2},{4,5},{5,4},{6,7},{7,6},{8,9},{9,8},{10,11... | collective-permute-start | bytes 4718600 | tf_op jit(solution)/shard_map/ppermute | solution.py:144
  72.1 8.7 %collective-permute-start.11 = (bf16[2,256,256]{2,1,0:T(8,128)(2,1)S(1)}, bf16[2,256,256]{2,1,0:T(8,128)(2,1)S(1)}, u32[]{:S(2)}, u32[]{:S(2)}) collective-permute-start(bf16[2,256,256]{2,1,0:T(8,128)(2,1)S(1)} %collective-permute-done.10.refs_2_), channel_id=1, source_target_pairs={{0,8},{4,12},{8,0},{12,4},{16,24},{20,28},{24,16},{28,20},{1,9},{5... | collective-permute-start | bytes 786440 | tf_op jit(solution)/shard_map/ppermute | solution.py:144
  82.4 6.5 %collective-permute-start.17 = (bf16[384,256]{1,0:T(8,128)(2,1)S(1)}, bf16[384,256]{1,0:T(8,128)(2,1)S(1)}, u32[]{:S(2)}, u32[]{:S(2)}) collective-permute-start(bf16[384,256]{1,0:T(8,128)(2,1)S(1)} %bitcast.32), channel_id=1, source_target_pairs={{0,4},{4,0},{8,12},{12,8},{16,20},{20,16},{24,28},{28,24},{1,5},{5... | collective-permute-start | bytes 589832 | tf_op jit(solution)/shard_map/ppermute | solution.py:144

commit v4 on v3

--- a/solution.py
+++ b/solution.py
@@ -125,6 +125,19 @@
         ref[...] = scaled(acc_ref[i * rows:(i + 1) * rows, :]).astype(ref.dtype)
 
 
+def split_kernel(here_ref, k, v, given_ref, mine_ref, sems):
+    lane = here_ref[0] % 2
+    copies = []
+    for i, (head, ref) in enumerate(((1 - lane, given_ref), (lane, mine_ref))):
+        columns = pl.ds(pl.multiple_of(head * HD, HD), HD)
+        copies.append(pltpu.make_async_copy(k.at[:, columns], ref.at[:, :HD], sems.at[2 * i]))
+        copies.append(pltpu.make_async_copy(v.at[:, columns], ref.at[:, HD:], sems.at[2 * i + 1]))
+    for copy in copies:
+        copy.start()
+    for copy in copies:
+        copy.wait()
+
+
 def called(kernel, name, operands, kinds, outs, scratch, mebibytes=44):
     places = {"s": pltpu.SMEM, "v": pltpu.VMEM, "h": pltpu.HBM, "a": pl.ANY}
     return pl.pallas_call(
@@ -153,11 +166,10 @@
         moved(kv_grads, "tok", lambda t, j=j: ((t // lanes) ^ j) * lanes + t % lanes) for j in range(1, heads)]
 
 
-def project_kernel(count, paired, picks_ref, *refs):
-    blocks, hids, (own_ref, away_ref) = refs[:count], refs[count:-2], refs[-2:]
+def line_rows(count, indices, paired, picks_ref, blocks, hids):
     line, head, mine = picks_ref[0], picks_ref[1], picks_ref[2]
     total = None
-    for j, block in enumerate(blocks):
+    for j, block in zip(indices, blocks):
         if paired:
             near = (line ^ j) % 2 == head % 2
             y = head // 2
@@ -175,6 +187,21 @@
         for turned, grads in terms:
             term = jnp.dot(turned, grads, preferred_element_type=jnp.float32)
             total = term if total is None else total + term
+    return total
+
+
+def part_kernel(indices, picks_ref, *refs):
+    n = len(indices)
+    refs[-1][...] = line_rows(4, indices, True, picks_ref, refs[:n], refs[n:-1])
+
+
+def project_kernel(count, indices, paired, picks_ref, *refs):
+    own_ref, away_ref = refs[-2:]
+    n = len(indices)
+    total = line_rows(count, indices, paired, picks_ref, refs[:n], refs[n:-3] if paired else refs[n:-2])
+    if paired:
+        total = total + refs[-3][...]
+    mine = picks_ref[2]
     lanes, part = away_ref.shape[0] + 1, own_ref.shape[0]
     own_ref[...] = jnp.zeros_like(own_ref)
     for d in range(lanes):
@@ -190,12 +217,17 @@
                 away_ref[e - 1] = piece.astype(jnp.bfloat16)
 
 
-def project(picks, hids, blocks, lanes):
-    part = hids[0].shape[-2] // lanes
-    columns = blocks[0].shape[-1]
+def project(picks, hids, blocks, lanes, indices=None, before=None):
+    rows, columns = hids[0].shape[-2], blocks[0].shape[-1]
+    part = rows // lanes
+    chosen_blocks = [blocks[j] for j in indices] if indices else blocks
+    operands = [*chosen_blocks, *hids] + ([] if before is None else [before])
+    if indices and before is None:
+        return called(functools.partial(part_kernel, indices), "part", [picks, *operands], "s" + "v" * len(operands),
+                      [((rows, columns), jnp.float32)], [])[0]
     return called(
-        functools.partial(project_kernel, len(blocks), len(hids) > 1), "project", [picks, *blocks, *hids],
-        "s" + "v" * (len(blocks) + len(hids)),
+        functools.partial(project_kernel, len(blocks), indices or range(len(blocks)), before is not None), "project",
+        [picks, *operands], "s" + "v" * len(operands),
         [((part, columns), jnp.float32), ((lanes - 1, part, columns), jnp.bfloat16)], [])
 
 
@@ -297,8 +329,8 @@
 
     y = head // 2
     half = rows // 2
-    given = jnp.where(even, stacked[1], stacked[0])
-    mine = jnp.where(even, after(stacked[0], given), stacked[1])
+    given, mine = called(split_kernel, "split", [place, *stacked], "shh", [((rows, 2 * HD), jnp.bfloat16)] * 2,
+                         [pltpu.SemaphoreType.DMA((4,))], 60)
     got = over(given)
     asked = over(jnp.stack([jnp.where(even, a[:, wide:], a[:, :wide]) for a in (after(x, given) for x in arrays)]))
     risen = jnp.stack([mine, got])
@@ -332,7 +364,9 @@
     blocks = [total, j1, across, moved(after(across, j1), "tok", lambda t: t ^ lanes)]
     hids = jnp.concatenate([after(hops, j1, across, sent), upright, beside, skew], axis=0)
     picks = jnp.stack([line, head, lane]).astype(jnp.int32)
-    kept, away = project(picks, [hids, moved(hids, "head", lambda h: h ^ 1)], blocks, lanes)
+    hids = [hids, moved(hids, "head", lambda h: h ^ 1)]
+    part = project(picks, hids, blocks, lanes, (0, 1, 2))
+    kept, away = project(picks, hids, blocks, lanes, (3,), part)
     came = over(away[0]).astype(jnp.float32)
     firsts, seconds = (jnp.concatenate(mine_and_other(made[l], sent[l]), axis=1) for l in range(2))
     return (firsts, seconds, jnp.concatenate(mine_and_other(kept, came), axis=1))
@@ -344,8 +378,12 @@
     lanes = tokens // heads
     here, head = lax.axis_index("tok"), lax.axis_index("head")
     arrays = (queries_first, queries_second, grads_first, grads_second)
-    stacked = [jnp.concatenate([x[:, c * HD:(c + 1) * HD] for x in (key_states, value_states)], axis=1) for c in range(kv_heads)]
-    plan = paired if (lanes, heads, kv_heads, REACH) == (2, 4, 2, 3) else general
+    if (lanes, heads, kv_heads, REACH) == (2, 4, 2, 3):
+        plan, stacked = paired, [key_states, value_states]
+    else:
+        plan = general
+        stacked = [jnp.concatenate([x[:, c * HD:(c + 1) * HD] for x in (key_states, value_states)], axis=1)
+                   for c in range(kv_heads)]
     return plan(here.reshape(1).astype(jnp.int32), here // lanes, here % lanes, head, heads, tokens, lanes, kv_heads,
                 doc_lengths, arrays, stacked, hidden_states)
 

time: 90.3 us -> 88.3 us (0.978)
  local copies, waits for them, and re-layouts: 3.98 us -> 1.4 us
  Pallas kernels: 13.3 us -> 15.8 us
  other arithmetic: 5.86 us -> 4.16 us
    pallas_call x3 -> x5, Pallas kernels: 13.3 us -> 15.8 us  [called(): pl.pallas_call(kernel, in_specs=[pl.BlockSpec(memory_space=places[k]) for...]
    slice x2 -> x0, local copies, waits for them, and re-layouts: 1.9 us -> none  [body(): x[:, c * HD:(c + 1) * HD]]
    select_n x1, other arithmetic: 1.02 us -> 0.09 us  [paired(): jnp.where(own_line, kept, lent)]
  transfers between devices with their start and end apart: 18 -> 18, of which waited for: 9 -> 10; matrix products, arithmetic and copies ran while one was open for 7% -> 5% of each run, Pallas kernels for 13% -> 15%
where the time goes in v4:
time: 88.3 us; the launch traced here: 88.1 us
  waiting for transfers between devices  37.7 us (43%)
  starting transfers between devices  28.1 us (32%)
  Pallas kernels  15.8 us (18%)
  other arithmetic  4.16 us (5%)
  local copies, waits for them, and re-layouts  1.4 us (2%)
  between operations  0.98 us (1%)
    ppermute x18, waiting for transfers between devices, moved(): lax.ppermute(value, axis, [(i, j) for i, j in pairs if j is not None])  37.7 us
    ppermute x18, starting transfers between devices, moved(): lax.ppermute(value, axis, [(i, j) for i, j in pairs if j is not None])  28.1 us
    pallas_call x5, Pallas kernels, called(): pl.pallas_call(kernel, in_specs=[pl.BlockSpec(memory_space=places[k]) for...  15.8 us
  transfers between devices with their start and end apart: 18, of which 10 were waited for; matrix products, arithmetic and copies ran while one was open for 5% of the time, Pallas kernels for 15%

profile of v4, /device:TPU:0, one launch (start us, length us, event | category | flops | bytes accessed | tf_op | source)
XLA Modules:
  0.0 88.1 jit_solution(15504071060597739813)
XLA Ops:
  0.7 1.8 %split.1 = (bf16[256,256]{1,0:T(8,128)(2,1)}, bf16[256,256]{1,0:T(8,128)(2,1)}) custom-call(s32[1]{0:T(128)} %bitcast.here_ref, bf16[256,256]{1,0:T(8,128)(2,1)} %k.1, bf16[256,256]{1,0:T(8,128)(2,1)} %v.1), custom_call_target="tpu_custom_call" | custom-call | flops 32768 | bytes 32768 | tf_op jit(solution)/shard_map/split/pallas_call | solution.py:143
  2.5 3.0 %collective-permute-start = (bf16[256,256]{1,0:T(8,128)(2,1)}, bf16[256,256]{1,0:T(8,128)(2,1)S(1)}, u32[]{:S(2)}, u32[]{:S(2)}) collective-permute-start(bf16[256,256]{1,0:T(8,128)(2,1)} %get-tuple-element.37), channel_id=1, source_target_pairs={{0,4},{4,0},{8,12},{12,8},{16,20},{20,16},{24,28},{28,24},{1,5},{5... | collective-permute-start | bytes 393224 | tf_op jit(solution)/shard_map/ppermute | solution.py:157
  5.5 1.2 %copy.11 = bf16[256,768]{0,1:T(8,128)(2,1)S(1)} copy(bf16[256,768]{1,0:T(8,128)(2,1)} %param.17) | data formatting | bytes 786432 | tf_op jit(solution)/shard_map/optimization_barrier | solution.py:161
  6.7 1.6 %collective-permute-start.4 = (bf16[128,768]{0,1:T(8,128)(2,1)S(1)}, bf16[128,768]{0,1:T(8,128)(2,1)S(1)}, u32[]{:S(2)}, u32[]{:S(2)}) collective-permute-start(bf16[128,768]{0,1:T(8,128)(2,1)S(1)} %constant_dynamic-slice_fusion), channel_id=1, source_target_pairs={{0,2},{1,3},{2,0},{3,1},{4,6},{5,7},{6,4},{7,5},{8,10},{9,11},{10,... | collective-permute-start | bytes 589832 | tf_op jit(solution)/shard_map/ppermute | solution.py:157
  10.0 3.5 %collective-permute-start.2 = (bf16[2,256,256]{2,1,0:T(8,128)(2,1)S(1)}, bf16[2,256,256]{2,1,0:T(8,128)(2,1)S(1)}, u32[]{:S(2)}, u32[]{:S(2)}) collective-permute-start(bf16[2,256,256]{2,1,0:T(8,128)(2,1)S(1)} %pad_maximum_fusion.4), channel_id=1, source_target_pairs={{0,8},{4,12},{8,16},{12,20},{16,24},{20,28},{1,9},{5,13},{9,17},{1... | collective-permute-start | bytes 786440 | tf_op jit(solution)/shard_map/ppermute | solution.py:157
  13.5 4.5 %collective-permute-start.1 = (bf16[256,256]{1,0:T(8,128)(2,1)S(1)}, bf16[256,256]{1,0:T(8,128)(2,1)S(1)}, u32[]{:S(2)}, u32[]{:S(2)}) collective-permute-start(bf16[256,256]{1,0:T(8,128)(2,1)S(1)} %broadcast_select_fusion.2), channel_id=1, source_target_pairs={{0,16},{4,20},{8,24},{12,28},{1,17},{5,21},{9,25},{13,29},{2,18},{... | collective-permute-start | bytes 393224 | tf_op jit(solution)/shard_map/ppermute | solution.py:157
  18.1 2.9 %collective-permute-done.1.far = bf16[256,256]{1,0:T(8,128)(2,1)S(1)} collective-permute-done((bf16[256,256]{1,0:T(8,128)(2,1)S(1)}, bf16[256,256]{1,0:T(8,128)(2,1)S(1)}, u32[]{:S(2)}, u32[]{:S(2)}) %collective-permute-start.1) | collective-permute-done | bytes 131104 | tf_op jit(solution)/shard_map/ppermute | solution.py:157
  21.0 4.8 %collective-permute-start.5 = (bf16[128,768]{0,1:T(8,128)(2,1)S(1)}, bf16[128,768]{0,1:T(8,128)(2,1)S(1)}, u32[]{:S(2)}, u32[]{:S(2)}) collective-permute-start(bf16[128,768]{0,1:T(8,128)(2,1)S(1)} %get-tuple-element.46), channel_id=1, source_target_pairs={{0,16},{1,24},{2,18},{3,26},{4,20},{5,28},{6,22},{7,30},{8,17},{9,... | collective-permute-start | bytes 589832 | tf_op jit(solution)/shard_map/ppermute | solution.py:157
  25.9 6.0 %attend_own.1 = (bf16[2,256,384]{2,1,0:T(8,128)(2,1)S(1)}, f32[1024,256]{1,0:T(8,128)S(1)}) custom-call(s32[1]{0:T(128)} %bitcast.here_ref, s32[8]{0:T(128)S(1)} %copy-done.5, bf16[256,768]{1,0:T(8,128)(2,1)S(1)} %copy-done.4, bf16[256,768]{1,0:T(8,128)(2,1)S(1)} %copy-done.3, bf16[256,768]{1,0:T(8,128)(2,1)S(1)} %copy-done.2, ...), custom_call_target="tpu_custom_call" | custom-call | flops 32768 | bytes 32768 | tf_op jit(solution)/shard_map/attend_own/pallas_call | solution.py:143
  32.6 2.6 %collective-permute-done.5 = bf16[128,768]{0,1:T(8,128)(2,1)S(1)} collective-permute-done((bf16[128,768]{0,1:T(8,128)(2,1)S(1)}, bf16[128,768]{0,1:T(8,128)(2,1)S(1)}, u32[]{:S(2)}, u32[]{:S(2)}) %collective-permute-start.5) | collective-permute-done | bytes 196640 | tf_op jit(solution)/shard_map/ppermute | solution.py:157
  35.2 5.8 %attend_other.1 = (bf16[2,256,384]{2,1,0:T(8,128)(2,1)S(1)}, bf16[256,256]{1,0:T(8,128)(2,1)S(1)}, bf16[2,256,256]{2,1,0:T(8,128)(2,1)S(1)}, f32[2,256,256]{2,1,0:T(8,128)S(1)}) custom-call(s32[1]{0:T(128)} %bitcast.here_ref, s32[8]{0:T(128)S(1)} %copy-done.5, bf16[4,256,384]{2,1,0:T(8,128)(2,1)S(1)} %collective-permute-done.3.held_ref, ...), custom_call_target="tpu_custom_call" | custom-call | flops 32768 | bytes 32768 | tf_op jit(solution)/shard_map/attend_other/pallas_call | solution.py:143
  41.0 1.5 %collective-permute-start.7 = (bf16[2,256,256]{2,1,0:T(8,128)(2,1)S(1)}, bf16[2,256,256]{2,1,0:T(8,128)(2,1)S(1)}, u32[]{:S(2)}, u32[]{:S(2)}) collective-permute-start(bf16[2,256,256]{2,1,0:T(8,128)(2,1)S(1)} %get-tuple-element.50), channel_id=1, source_target_pairs={{8,0},{12,4},{16,8},{20,12},{24,16},{28,20},{9,1},{13,5},{17,9},{2... | collective-permute-start | bytes 786440 | tf_op jit(solution)/shard_map/ppermute | solution.py:157
  42.5 1.6 %collective-permute-start.14 = (bf16[2,768,128]{2,1,0:T(8,128)(2,1)S(1)}, bf16[2,768,128]{2,1,0:T(8,128)(2,1)S(1)}, u32[]{:S(2)}, u32[]{:S(2)}) collective-permute-start(bf16[2,768,128]{2,1,0:T(8,128)(2,1)S(1)} %maximum_bitcast_fusion), channel_id=1, source_target_pairs={{0,4},{4,0},{8,12},{12,8},{16,20},{20,16},{24,28},{28,24},{1,5},{5... | collective-permute-start | bytes 1179656 | tf_op jit(solution)/shard_map/ppermute | solution.py:157
  45.0 1.3 %collective-permute-start.8 = (bf16[256,256]{1,0:T(8,128)(2,1)S(1)}, bf16[256,256]{1,0:T(8,128)(2,1)S(1)}, u32[]{:S(2)}, u32[]{:S(2)}) collective-permute-start(bf16[256,256]{1,0:T(8,128)(2,1)S(1)} %get-tuple-element.51), channel_id=1, source_target_pairs={{16,0},{20,4},{24,8},{28,12},{17,1},{21,5},{25,9},{29,13},{18,2},{... | collective-permute-start | bytes 393224 | tf_op jit(solution)/shard_map/ppermute | solution.py:157
  46.9 6.7 %collective-permute-done.7 = bf16[2,256,256]{2,1,0:T(8,128)(2,1)S(1)} collective-permute-done((bf16[2,256,256]{2,1,0:T(8,128)(2,1)S(1)}, bf16[2,256,256]{2,1,0:T(8,128)(2,1)S(1)}, u32[]{:S(2)}, u32[]{:S(2)}) %collective-permute-start.7) | collective-permute-done | bytes 262176 | tf_op jit(solution)/shard_map/ppermute | solution.py:157
  53.6 3.4 %collective-permute-done.8 = bf16[256,256]{1,0:T(8,128)(2,1)S(1)} collective-permute-done((bf16[256,256]{1,0:T(8,128)(2,1)S(1)}, bf16[256,256]{1,0:T(8,128)(2,1)S(1)}, u32[]{:S(2)}, u32[]{:S(2)}) %collective-permute-start.8) | collective-permute-done | bytes 131104 | tf_op jit(solution)/shard_map/ppermute | solution.py:157
  58.4 4.5 %collective-permute-done.6 = bf16[2,256,384]{2,1,0:T(8,128)(2,1)S(1)} collective-permute-done((bf16[2,256,384]{2,1,0:T(8,128)(2,1)S(1)}, bf16[2,256,384]{2,1,0:T(8,128)(2,1)S(1)}, u32[]{:S(2)}, u32[]{:S(2)}) %collective-permute-start.6) | collective-permute-done | bytes 393248 | tf_op jit(solution)/shard_map/ppermute | solution.py:157
  62.9 4.3 %collective-permute-done.10.refs_1_ = bf16[2,256,256]{2,1,0:T(8,128)(2,1)S(1)} collective-permute-done((bf16[2,256,256]{2,1,0:T(8,128)(2,1)S(1)}, bf16[2,256,256]{2,1,0:T(8,128)(2,1)S(1)}, u32[]{:S(2)}, u32[]{:S(2)}) %collective-permute-start.10) | collective-permute-done | bytes 262176 | tf_op jit(solution)/shard_map/ppermute | solution.py:157
  67.2 2.9 %collective-permute-done.9.refs_2_ = bf16[2,256,256]{2,1,0:T(8,128)(2,1)S(1)} collective-permute-done((bf16[2,256,256]{2,1,0:T(8,128)(2,1)S(1)}, bf16[2,256,256]{2,1,0:T(8,128)(2,1)S(1)}, u32[]{:S(2)}, u32[]{:S(2)}) %collective-permute-start.9) | collective-permute-done | bytes 262176 | tf_op jit(solution)/shard_map/ppermute | solution.py:157
  70.7 3.2 %collective-permute-done.16.refs_4_.refs_2_ = bf16[8,768,128]{2,1,0:T(8,128)(2,1)S(1)} collective-permute-done((bf16[8,768,128]{2,1,0:T(8,128)(2,1)S(1)}, bf16[8,768,128]{2,1,0:T(8,128)(2,1)S(1)}, u32[]{:S(2)}, u32[]{:S(2)}) %collective-permute-start.16) | collective-permute-done | bytes 1572896 | tf_op jit(solution)/shard_map/ppermute | solution.py:157
  73.8 1.3 %part.1.refs_3_ = f32[768,256]{1,0:T(8,128)S(1)} custom-call(s32[3]{0:T(128)S(1)} %pad_add_fusion.picks_ref, bf16[2,256,256]{2,1,0:T(8,128)(2,1)S(1)} %convert_element_type.11.refs_0_, bf16[2,256,256]{2,1,0:T(8,128)(2,1)S(1)} %collective-permute-done.10.refs_1_, bf16[2,256,256]{2,1,0:T(8,128)(2,1)S(1)} %collective-permute-done.9.refs_2_, ...), custom_call_target="tpu_custom_call" | custom-call | flops 32768 | bytes 32768 | tf_op jit(solution)/shard_map/part/pallas_call | solution.py:143
  75.2 4.0 %collective-permute-done.11.refs_0_ = bf16[2,256,256]{2,1,0:T(8,128)(2,1)S(1)} collective-permute-done((bf16[2,256,256]{2,1,0:T(8,128)(2,1)S(1)}, bf16[2,256,256]{2,1,0:T(8,128)(2,1)S(1)}, u32[]{:S(2)}, u32[]{:S(2)}) %collective-permute-start.11) | collective-permute-done | bytes 262176 | tf_op jit(solution)/shard_map/ppermute | solution.py:157
  80.1 2.2 %collective-permute-start.17 = (bf16[384,256]{1,0:T(8,128)(2,1)S(1)}, bf16[384,256]{1,0:T(8,128)(2,1)S(1)}, u32[]{:S(2)}, u32[]{:S(2)}) collective-permute-start(bf16[384,256]{1,0:T(8,128)(2,1)S(1)} %bitcast.32), channel_id=1, source_target_pairs={{0,4},{4,0},{8,12},{12,8},{16,20},{20,16},{24,28},{28,24},{1,5},{5... | collective-permute-start | bytes 589832 | tf_op jit(solution)/shard_map/ppermute | solution.py:157
  83.8 3.2 %collective-permute-done.17 = bf16[384,256]{1,0:T(8,128)(2,1)S(1)} collective-permute-done((bf16[384,256]{1,0:T(8,128)(2,1)S(1)}, bf16[384,256]{1,0:T(8,128)(2,1)S(1)}, u32[]{:S(2)}, u32[]{:S(2)}) %collective-permute-start.17) | collective-permute-done | bytes 196640 | tf_op jit(solution)/shard_map/ppermute | solution.py:157
  (51 shorter events, 9.5 us)
Async XLA Ops:
  0.6 7.6 %copy-start.4 = (bf16[256,768]{1,0:T(8,128)(2,1)S(1)}, bf16[256,768]{1,0:T(8,128)(2,1)}, u32[]{:S(2)}) copy-start(bf16[256,768]{1,0:T(8,128)(2,1)} %q1.1) | copy-start | bytes 1179652
  0.6 7.6 %copy-start.3 = (bf16[256,768]{1,0:T(8,128)(2,1)S(1)}, bf16[256,768]{1,0:T(8,128)(2,1)}, u32[]{:S(2)}) copy-start(bf16[256,768]{1,0:T(8,128)(2,1)} %q2.1) | copy-start | bytes 1179652
  0.7 7.7 %copy-start.2 = (bf16[256,768]{1,0:T(8,128)(2,1)S(1)}, bf16[256,768]{1,0:T(8,128)(2,1)}, u32[]{:S(2)}) copy-start(bf16[256,768]{1,0:T(8,128)(2,1)} %g1.1) | copy-start | bytes 1179652
  0.7 7.7 %copy-start.1 = (bf16[256,768]{1,0:T(8,128)(2,1)S(1)}, bf16[256,768]{1,0:T(8,128)(2,1)}, u32[]{:S(2)}) copy-start(bf16[256,768]{1,0:T(8,128)(2,1)} %g2.1) | copy-start | bytes 1179652
  2.5 7.5 %collective-permute-start = (bf16[256,256]{1,0:T(8,128)(2,1)}, bf16[256,256]{1,0:T(8,128)(2,1)S(1)}, u32[]{:S(2)}, u32[]{:S(2)}) collective-permute-start(bf16[256,256]{1,0:T(8,128)(2,1)} %get-tuple-element.37), channel_id=1, source_target_pairs={{0,4},{4,0},{8,12},{12,8},{16,20},{20,16},{24,28},{28,24},{1,5},{5... | collective-permute-start | bytes 393224 | tf_op jit(solution)/shard_map/ppermute | solution.py:157
  6.7 11.4 %collective-permute-start.4 = (bf16[128,768]{0,1:T(8,128)(2,1)S(1)}, bf16[128,768]{0,1:T(8,128)(2,1)S(1)}, u32[]{:S(2)}, u32[]{:S(2)}) collective-permute-start(bf16[128,768]{0,1:T(8,128)(2,1)S(1)} %constant_dynamic-slice_fusion), channel_id=1, source_target_pairs={{0,2},{1,3},{2,0},{3,1},{4,6},{5,7},{6,4},{7,5},{8,10},{9,11},{10,... | collective-permute-start | bytes 589832 | tf_op jit(solution)/shard_map/ppermute | solution.py:157
  8.3 1.6 %copy-start = (bf16[256,256]{1,0:T(8,128)(2,1)S(1)}, bf16[256,256]{1,0:T(8,128)(2,1)}, u32[]{:S(2)}) copy-start(bf16[256,256]{1,0:T(8,128)(2,1)} %get-tuple-element.38.mine) | copy-start | bytes 393220
  8.4 17.5 %copy-start.5 = (s32[8]{0:T(128)S(1)}, s32[8]{0:T(128)}, u32[]{:S(2)}) copy-start(s32[8]{0:T(128)} %lens_ref.3) | copy-start | bytes 100
  9.4 25.8 %collective-permute-start.3 = (bf16[4,256,384]{2,1,0:T(8,128)(2,1)}, bf16[4,256,384]{2,1,0:T(8,128)(2,1)S(1)}, u32[]{:S(2)}, u32[]{:S(2)}) collective-permute-start(bf16[4,256,384]{2,1,0:T(8,128)(2,1)} %pad_maximum_fusion), channel_id=1, source_target_pairs={{0,4},{4,0},{8,12},{12,8},{16,20},{20,16},{24,28},{28,24},{1,5},{5... | collective-permute-start | bytes 2359304 | tf_op jit(solution)/shard_map/ppermute | solution.py:157
  10.0 11.1 %collective-permute-start.2 = (bf16[2,256,256]{2,1,0:T(8,128)(2,1)S(1)}, bf16[2,256,256]{2,1,0:T(8,128)(2,1)S(1)}, u32[]{:S(2)}, u32[]{:S(2)}) collective-permute-start(bf16[2,256,256]{2,1,0:T(8,128)(2,1)S(1)} %pad_maximum_fusion.4), channel_id=1, source_target_pairs={{0,8},{4,12},{8,16},{12,20},{16,24},{20,28},{1,9},{5,13},{9,17},{1... | collective-permute-start | bytes 786440 | tf_op jit(solution)/shard_map/ppermute | solution.py:157
  13.5 7.5 %collective-permute-start.1 = (bf16[256,256]{1,0:T(8,128)(2,1)S(1)}, bf16[256,256]{1,0:T(8,128)(2,1)S(1)}, u32[]{:S(2)}, u32[]{:S(2)}) collective-permute-start(bf16[256,256]{1,0:T(8,128)(2,1)S(1)} %broadcast_select_fusion.2), channel_id=1, source_target_pairs={{0,16},{4,20},{8,24},{12,28},{1,17},{5,21},{9,25},{13,29},{2,18},{... | collective-permute-start | bytes 393224 | tf_op jit(solution)/shard_map/ppermute | solution.py:157
  21.0 14.2 %collective-permute-start.5 = (bf16[128,768]{0,1:T(8,128)(2,1)S(1)}, bf16[128,768]{0,1:T(8,128)(2,1)S(1)}, u32[]{:S(2)}, u32[]{:S(2)}) collective-permute-start(bf16[128,768]{0,1:T(8,128)(2,1)S(1)} %get-tuple-element.46), channel_id=1, source_target_pairs={{0,16},{1,24},{2,18},{3,26},{4,20},{5,28},{6,22},{7,30},{8,17},{9,... | collective-permute-start | bytes 589832 | tf_op jit(solution)/shard_map/ppermute | solution.py:157
  31.9 10.6 %collective-permute-start.12 = (bf16[128,768]{0,1:T(8,128)(2,1)S(1)}, bf16[128,768]{0,1:T(8,128)(2,1)S(1)}, u32[]{:S(2)}, u32[]{:S(2)}) collective-permute-start(bf16[128,768]{0,1:T(8,128)(2,1)S(1)} %get-tuple-element.53), channel_id=1, source_target_pairs={{0,0},{1,8},{2,2},{3,10},{4,4},{5,12},{6,6},{7,14},{8,1},{9,9},{10... | collective-permute-start | bytes 589832 | tf_op jit(solution)/shard_map/ppermute | solution.py:157
  41.0 12.6 %collective-permute-start.7 = (bf16[2,256,256]{2,1,0:T(8,128)(2,1)S(1)}, bf16[2,256,256]{2,1,0:T(8,128)(2,1)S(1)}, u32[]{:S(2)}, u32[]{:S(2)}) collective-permute-start(bf16[2,256,256]{2,1,0:T(8,128)(2,1)S(1)} %get-tuple-element.50), channel_id=1, source_target_pairs={{8,0},{12,4},{16,8},{20,12},{24,16},{28,20},{9,1},{13,5},{17,9},{2... | collective-permute-start | bytes 786440 | tf_op jit(solution)/shard_map/ppermute | solution.py:157
  42.5 14.7 %collective-permute-start.14 = (bf16[2,768,128]{2,1,0:T(8,128)(2,1)S(1)}, bf16[2,768,128]{2,1,0:T(8,128)(2,1)S(1)}, u32[]{:S(2)}, u32[]{:S(2)}) collective-permute-start(bf16[2,768,128]{2,1,0:T(8,128)(2,1)S(1)} %maximum_bitcast_fusion), channel_id=1, source_target_pairs={{0,4},{4,0},{8,12},{12,8},{16,20},{20,16},{24,28},{28,24},{1,5},{5... | collective-permute-start | bytes 1179656 | tf_op jit(solution)/shard_map/ppermute | solution.py:157
  44.1 26.1 %collective-permute-start.13 = (bf16[2,768,128]{2,1,0:T(8,128)(2,1)S(1)}, bf16[2,768,128]{2,1,0:T(8,128)(2,1)S(1)}, u32[]{:S(2)}, u32[]{:S(2)}) collective-permute-start(bf16[2,768,128]{2,1,0:T(8,128)(2,1)S(1)} %maximum_bitcast_fusion), channel_id=1, source_target_pairs={{0,2},{1,3},{2,0},{3,1},{4,6},{5,7},{6,4},{7,5},{8,10},{9,11},{10,... | collective-permute-start | bytes 1179656 | tf_op jit(solution)/shard_map/ppermute | solution.py:157
  45.0 12.0 %collective-permute-start.8 = (bf16[256,256]{1,0:T(8,128)(2,1)S(1)}, bf16[256,256]{1,0:T(8,128)(2,1)S(1)}, u32[]{:S(2)}, u32[]{:S(2)}) collective-permute-start(bf16[256,256]{1,0:T(8,128)(2,1)S(1)} %get-tuple-element.51), channel_id=1, source_target_pairs={{16,0},{20,4},{24,8},{28,12},{17,1},{21,5},{25,9},{29,13},{18,2},{... | collective-permute-start | bytes 393224 | tf_op jit(solution)/shard_map/ppermute | solution.py:157
  46.3 16.6 %collective-permute-start.6 = (bf16[2,256,384]{2,1,0:T(8,128)(2,1)S(1)}, bf16[2,256,384]{2,1,0:T(8,128)(2,1)S(1)}, u32[]{:S(2)}, u32[]{:S(2)}) collective-permute-start(bf16[2,256,384]{2,1,0:T(8,128)(2,1)S(1)} %get-tuple-element.48), channel_id=1, source_target_pairs={{0,4},{4,0},{8,12},{12,8},{16,20},{20,16},{24,28},{28,24},{1,5},{5... | collective-permute-start | bytes 1179656 | tf_op jit(solution)/shard_map/ppermute | solution.py:157
  57.1 10.1 %collective-permute-start.10 = (bf16[2,256,256]{2,1,0:T(8,128)(2,1)S(1)}, bf16[2,256,256]{2,1,0:T(8,128)(2,1)S(1)}, u32[]{:S(2)}, u32[]{:S(2)}) collective-permute-start(bf16[2,256,256]{2,1,0:T(8,128)(2,1)S(1)} %convert_element_type.11.refs_0_), channel_id=1, source_target_pairs={{0,8},{4,12},{8,0},{12,4},{16,24},{20,28},{24,16},{28,20},{1,9},{5... | collective-permute-start | bytes 786440 | tf_op jit(solution)/shard_map/ppermute | solution.py:157
  57.2 13.0 %collective-permute-start.9 = (bf16[2,256,256]{2,1,0:T(8,128)(2,1)S(1)}, bf16[2,256,256]{2,1,0:T(8,128)(2,1)S(1)}, u32[]{:S(2)}, u32[]{:S(2)}) collective-permute-start(bf16[2,256,256]{2,1,0:T(8,128)(2,1)S(1)} %convert_element_type.11.refs_0_), channel_id=1, source_target_pairs={{0,16},{4,20},{8,24},{12,28},{16,0},{20,4},{24,8},{28,12},{1,17},{... | collective-permute-start | bytes 786440 | tf_op jit(solution)/shard_map/ppermute | solution.py:157
  57.3 13.0 %collective-permute-start.15 = (bf16[2,768,128]{2,1,0:T(8,128)(2,1)S(1)}, bf16[2,768,128]{2,1,0:T(8,128)(2,1)S(1)}, u32[]{:S(2)}, u32[]{:S(2)}) collective-permute-start(bf16[2,768,128]{2,1,0:T(8,128)(2,1)S(1)} %collective-permute-done.14), channel_id=1, source_target_pairs={{0,2},{1,3},{2,0},{3,1},{4,6},{5,7},{6,4},{7,5},{8,10},{9,11},{10,... | collective-permute-start | bytes 1179656 | tf_op jit(solution)/shard_map/ppermute | solution.py:157
  70.4 3.5 %collective-permute-start.16 = (bf16[8,768,128]{2,1,0:T(8,128)(2,1)S(1)}, bf16[8,768,128]{2,1,0:T(8,128)(2,1)S(1)}, u32[]{:S(2)}, u32[]{:S(2)}) collective-permute-start(bf16[8,768,128]{2,1,0:T(8,128)(2,1)S(1)} %constant_dynamic-update-slice_fusion.refs_3_.refs_1_), channel_id=1, source_target_pairs={{0,1},{1,0},{2,3},{3,2},{4,5},{5,4},{6,7},{7,6},{8,9},{9,8},{10,11... | collective-permute-start | bytes 4718600 | tf_op jit(solution)/shard_map/ppermute | solution.py:157
  70.4 8.7 %collective-permute-start.11 = (bf16[2,256,256]{2,1,0:T(8,128)(2,1)S(1)}, bf16[2,256,256]{2,1,0:T(8,128)(2,1)S(1)}, u32[]{:S(2)}, u32[]{:S(2)}) collective-permute-start(bf16[2,256,256]{2,1,0:T(8,128)(2,1)S(1)} %collective-permute-done.9.refs_2_), channel_id=1, source_target_pairs={{0,8},{4,12},{8,0},{12,4},{16,24},{20,28},{24,16},{28,20},{1,9},{5... | collective-permute-start | bytes 786440 | tf_op jit(solution)/shard_map/ppermute | solution.py:157
  80.1 6.9 %collective-permute-start.17 = (bf16[384,256]{1,0:T(8,128)(2,1)S(1)}, bf16[384,256]{1,0:T(8,128)(2,1)S(1)}, u32[]{:S(2)}, u32[]{:S(2)}) collective-permute-start(bf16[384,256]{1,0:T(8,128)(2,1)S(1)} %bitcast.32), channel_id=1, source_target_pairs={{0,4},{4,0},{8,12},{12,8},{16,20},{20,16},{24,28},{28,24},{1,5},{5... | collective-permute-start | bytes 589832 | tf_op jit(solution)/shard_map/ppermute | solution.py:157
